TPU v7x, 512 devices: a whole 4x8x8 slice. The times are simulated.
512 devices in a mesh: tile: 128 (over y, z, core), lev: 4 (over x).
Axes of the slice: x: 4, y: 8, z: 8, core: 2. Of those that a mesh axis runs over, the one named last changes fastest.
Arguments:
- tracers: float32 [4, 16, 4096, 384], P(None, 'lev', 'tile'), may hold values from -6 to 6
- u_courant: float32 [16, 4096, 384], P('lev', 'tile'), may hold values from -0.3 to 0.3
- v_courant: float32 [16, 4096, 384], P('lev', 'tile'), may hold values from -0.3 to 0.3
- w_courant: float32 [16, 4096, 384], P('lev', 'tile'), may hold values from -0.3 to 0.3
- land_mask: int32 [4096, 384], P('tile'), may hold values 0 or 1
- weights: bfloat16 [8, 512, 256], replicated, may hold values from -0.078125 to 0.078125
- src_block: int32 [16384], P('tile'), may hold values from 0 to 23
- dst_tile: int32 [16384, 1], P('tile'), may hold values from 0 to 127; in each aligned block of 128 rows (0 to 127, 128 to 255, ...) at most 2 rows name the same one
- dst_block: int32 [16384], P('tile'), may hold values from 0 to 15
- pattern: int32 [16384], P('tile'), may hold values from 0 to 7
Outputs:
- new_tracers: float32 [4, 16, 4096, 384], P(None, 'lev', 'tile')
- target_fields: float32 [4, 16, 524288], P(None, 'lev', 'tile')
- target_flux: float32 [4, 16, 524288], P(None, 'lev', 'tile')
Inputs may be any that keep to these rules, and one draw needn't show every extreme that they name: `dst_tile`: among the 128 entries of one strip no target strip is named more than 2 times, and some target strip is named exactly 2 times.
All inputs are finite; a program needn't handle non-finite values. No bound on the sum of `land_mask` on one device may be relied on, other than what follows from the above.
Results may differ from a plain program's by a relative error of at most 0.0041.
Values may be sent and summed in bfloat16 or wider, within the bound.
A program may use at most 128 MiB of HBM per device.

v0:
```python
import jax
import jax.numpy as jnp
from jax import lax
from jax.sharding import PartitionSpec as P

NBD = 16


def padded(shard, sides, width, wrap):
    for axis, dim in sides:
        peers, length = (lax.axis_size(axis), shard.shape[dim])
        up = [(i, (i + 1) % peers) for i in range(peers if wrap else peers - 1)]
        down = [(j, i) for i, j in up]
        last = lax.slice_in_dim(shard, length - width, length, axis=dim)
        leading = lax.slice_in_dim(shard, 0, width, axis=dim)
        before = lax.ppermute(last, axis, up)
        after = lax.ppermute(leading, axis, down)
        shard = jnp.concatenate([before, shard, after], axis=dim)
    return shard


def partner(block, axis, stride):
    count = lax.axis_size(axis)
    route = []
    for low in range(count):
        high = low | 1 << stride
        if high != low and high < count:
            route += [(low, high), (high, low)]
    return lax.ppermute(block, axis, route)


def minmod(first, second):
    return jnp.where(
        first * second > 0.0, jnp.sign(first) * jnp.minimum(jnp.abs(first), jnp.abs(second)), 0.0
    )


def face_flux(behind, left_cell, right_cell, beyond, courant, opening):
    left_slope = minmod(left_cell - behind, right_cell - left_cell)
    right_slope = minmod(right_cell - left_cell, beyond - right_cell)
    upwind = jnp.maximum(courant, 0.0) * (left_cell + 0.5 * (1.0 - courant) * left_slope)
    downwind = jnp.minimum(courant, 0.0) * (right_cell - 0.5 * (1.0 + courant) * right_slope)
    return opening * (upwind + downwind)


def apply_weights(blocks, kind_ids, weights):
    group_size = 16
    entry_count = blocks.shape[0]
    grouped = blocks.reshape((entry_count // group_size, group_size) + blocks.shape[1:])
    kind_groups = kind_ids.reshape(entry_count // group_size, group_size)

    def one_group(members):
        block_group, kind_group = members
        matrices = jnp.take(weights, kind_group, axis=0)
        products = jnp.einsum(
            "erc,ecd->erd", block_group, matrices, preferred_element_type=jnp.float32
        )
        return products.astype(jnp.bfloat16)

    result = lax.map(one_group, (grouped, kind_groups))
    return result.reshape((entry_count,) + result.shape[2:])


def shards(
    tracers,
    u_courant,
    v_courant,
    w_courant,
    land_mask,
    weights,
    src_block,
    dst_tile,
    dst_block,
    pattern,
):
    tracer_count, levels_dev, columns, rows_dev = tracers.shape
    ocean = land_mask.astype(jnp.float32)
    ocean_levels = jnp.broadcast_to(ocean[None, None], (1, levels_dev, columns, rows_dev))
    lateral = jnp.concatenate([tracers, ocean_levels, u_courant[None]], 0)
    widened = padded(lateral, (("tile", 2),), 2, True)
    side_cells = widened[:tracer_count]
    side_ocean = widened[tracer_count, 0]
    side_courant = widened[tracer_count + 1]
    east_faces = face_flux(
        side_cells[:, :, 0 : columns + 1],
        side_cells[:, :, 1 : columns + 2],
        side_cells[:, :, 2 : columns + 3],
        side_cells[:, :, 3 : columns + 4],
        side_courant[:, 1 : columns + 2],
        side_ocean[1 : columns + 2] * side_ocean[2 : columns + 3],
    )
    east_flux = east_faces[:, :, 1:]
    west_flux = east_faces[:, :, :columns]
    top_rows = jnp.concatenate(
        [
            tracers[..., rows_dev - 2 :],
            ocean_levels[..., rows_dev - 2 :],
            v_courant[None, :, :, rows_dev - 2 :],
        ],
        0,
    )
    partner_rows = top_rows
    for bit_number in range(lax.axis_size("tile").bit_length() - 1):
        partner_rows = partner(partner_rows, "tile", bit_number)
    mirrored = jnp.flip(partner_rows, (2, 3))
    ghost_cells = mirrored[:tracer_count]
    ghost_ocean = mirrored[tracer_count, 0, :, 0]
    ghost_courant = mirrored[tracer_count + 1, :, :, 0]
    zero_row = jnp.zeros((tracer_count, levels_dev, columns, 1), jnp.float32)
    extended = jnp.concatenate([zero_row, tracers, ghost_cells], 3)
    top_courant = 0.5 * (v_courant[:, :, rows_dev - 1] - ghost_courant)
    north_courant = jnp.concatenate([v_courant[:, :, : rows_dev - 1], top_courant[:, :, None]], 2)
    top_open = ocean[:, rows_dev - 1] * ghost_ocean
    north_open = jnp.concatenate([ocean[:, : rows_dev - 1] * ocean[:, 1:], top_open[:, None]], 1)
    north_flux = face_flux(
        extended[..., 0:rows_dev],
        extended[..., 1 : rows_dev + 1],
        extended[..., 2 : rows_dev + 2],
        extended[..., 3 : rows_dev + 3],
        north_courant,
        north_open,
    )
    south_flux = jnp.concatenate([zero_row, north_flux[..., : rows_dev - 1]], 3)
    vertical = jnp.concatenate([tracers, w_courant[None]], 0)
    deepened = padded(vertical, (("lev", 1),), 2, False)
    column_cells = deepened[:tracer_count]
    column_courant = deepened[tracer_count]
    all_levels = levels_dev * lax.axis_size("lev")
    level_global = (
        lax.axis_index("lev") * levels_dev + jnp.arange(levels_dev + 1, dtype=jnp.int32) - 1
    )
    level_open = (level_global < all_levels - 1).astype(jnp.float32)
    below_faces = face_flux(
        column_cells[:, 0 : levels_dev + 1],
        column_cells[:, 1 : levels_dev + 2],
        column_cells[:, 2 : levels_dev + 3],
        column_cells[:, 3 : levels_dev + 4],
        column_courant[1 : levels_dev + 2],
        ocean[None] * level_open[:, None, None],
    )
    below_flux = below_faces[:, 1:]
    above_flux = below_faces[:, :levels_dev]
    divergence = east_flux - west_flux + (north_flux - south_flux) + (below_flux - above_flux)
    new_tracers = tracers - divergence
    payload = jnp.stack([new_tracers, divergence]).astype(jnp.bfloat16)
    row_count = 2 * tracer_count * levels_dev
    block_size = weights.shape[1]
    source_blocks = payload.reshape(
        row_count, columns * rows_dev // block_size, block_size
    ).transpose(1, 0, 2)
    strips = lax.axis_size("tile")
    capacity = max(2, 2 * src_block.shape[0] // strips)
    slot_count = strips * capacity
    targets = dst_tile[:, 0]
    owner_hits = (targets[:, None] == jnp.arange(strips, dtype=jnp.int32)[None, :]).astype(
        jnp.int32
    )
    slot_ranks = jnp.sum(jnp.cumsum(owner_hits, 0) * owner_hits, 1) - 1
    slot_index = targets * capacity + slot_ranks
    slot_blocks = (
        jnp.full((slot_count,), -1, jnp.int32)
        .at[slot_index]
        .set(dst_block)
        .reshape(strips, capacity)
    )
    raw_blocks = (
        jnp.zeros((slot_count, row_count, block_size), jnp.bfloat16)
        .at[slot_index]
        .set(source_blocks[src_block])
    )
    slot_kinds = (
        jnp.zeros((slot_count,), jnp.int32).at[slot_index].set(pattern).reshape(strips, capacity)
    )
    arrived, arrived_blocks, arrived_kinds = (
        lax.all_to_all(
            raw_blocks.reshape(strips, capacity, row_count, block_size),
            "tile",
            split_axis=0,
            concat_axis=0,
            tiled=True,
        ),
        lax.all_to_all(slot_blocks, "tile", split_axis=0, concat_axis=0, tiled=True),
        lax.all_to_all(slot_kinds, "tile", split_axis=0, concat_axis=0, tiled=True),
    )
    slot_terms = apply_weights(
        arrived.reshape(slot_count, row_count, block_size),
        arrived_kinds.reshape(slot_count),
        weights,
    )
    block_hits = (
        arrived_blocks.reshape(slot_count)[None, :] == jnp.arange(NBD, dtype=jnp.int32)[:, None]
    ).astype(jnp.bfloat16)
    summed = jnp.dot(
        block_hits, slot_terms.reshape(slot_count, -1), preferred_element_type=jnp.float32
    )
    shaped = summed.reshape(NBD, 2, tracer_count, levels_dev, -1).transpose(1, 2, 3, 0, 4)
    shaped = shaped.reshape(2, tracer_count, levels_dev, -1)
    return (new_tracers, shaped[0], shaped[1])


def solution(mesh):
    in_specs = (
        P(None, "lev", "tile", None),
        P("lev", "tile", None),
        P("lev", "tile", None),
        P("lev", "tile", None),
        P("tile", None),
        P(),
        P("tile"),
        P("tile", None),
        P("tile"),
        P("tile"),
    )
    out_specs = (P(None, "lev", "tile", None), P(None, "lev", "tile"), P(None, "lev", "tile"))
    return jax.shard_map(shards, mesh=mesh, in_specs=in_specs, out_specs=out_specs, check_vma=False)
```

profile of v0, /device:TPU:107, one launch (start us, length us, event | category | flops | bytes accessed | tf_op | source)
XLA Modules:
  0.0 539.9 jit_solution(16660333112355442692)
XLA Ops:
  3.0 4.6 collective-permute-start
  11.7 3.1 collective-permute-start.9
  20.6 8.8 %collective-permute-start.3 = (f32[6,4,32,2]{2,1,3,0:T(4,128)S(1)}, f32[6,4,32,2]{2,1,3,0:T(4,128)S(1)}, u32[]{:S(2)}, u32[]{:S(2)}) collective-permute-start(f32[6,4,32,2]{2,1,3,0:T(4,128)S(1)} %collective-permute-done.2), channel_id=1, source_target_pairs={{0,8},{8,0},{4,12},{12,4},{16,24},{24,16},{20,28},{28,20},{32,40},... | collective-permute-start | bytes 18440 | tf_op jit(solution)/shard_map/ppermute | solution.py:29
  31.3 11.3 %all-to-all-start.2 = ((s32[128,1,2]{2,1,0:T(1,128)}), s32[128,1,2]{2,1,0:T(1,128)S(1)}, u32[]{:S(2)}, u32[]{:S(2)}) async-start(s32[128,1,2]{2,1,0:T(1,128)} %bitcast.27), calls=%async_computation.2 | async-start | bytes 131072 | tf_op jit(solution)/shard_map/all_to_all | solution.py:183
  42.6 4.0 collective-permute-start.4
  48.5 5.8 %collective-permute-start.5 = (f32[6,4,32,2]{2,1,3,0:T(4,128)S(1)}, f32[6,4,32,2]{2,1,3,0:T(4,128)S(1)}, u32[]{:S(2)}, u32[]{:S(2)}) collective-permute-start(f32[6,4,32,2]{2,1,3,0:T(4,128)S(1)} %collective-permute-done.4), channel_id=1, source_target_pairs={{0,32},{32,0},{4,36},{36,4},{8,40},{40,8},{12,44},{44,12},{16,48},... | collective-permute-start | bytes 18440 | tf_op jit(solution)/shard_map/ppermute | solution.py:29
  57.0 3.0 collective-permute-start.6
  64.0 3.1 collective-permute-done.7
  71.9 3.9 collective-permute-done.8
  83.8 19.3 %all-to-all-start = ((s32[128,1,2]{2,1,0:T(1,128)}), s32[128,1,2]{2,1,0:T(1,128)S(1)}, u32[]{:S(2)}, u32[]{:S(2)}) async-start(s32[128,1,2]{2,1,0:T(1,128)} %bitcast.19), calls=%async_computation | async-start | bytes 131072 | tf_op jit(solution)/shard_map/all_to_all | solution.py:182
  106.8 4.3 broadcast_in_dim.50
  111.1 19.7 %scatter_fusion = bf16[256,32,512]{2,1,0:T(8,128)(2,1)} fusion(bf16[256,32,512]{2,1,0:T(8,128)(2,1)} %broadcast_in_dim.50, s32[128]{0:T(128)S(1)} %fusion.35, bf16[128,32,512]{2,1,0:T(8,128)(2,1)} %gather_fusion.1), kind=kCustom, calls=%fused_computation.3 | custom fusion | bytes 12583424 | tf_op jit(solution)/shard_map/scatter | solution.py:169
  130.8 14.3 %all-to-all-start.1 = ((bf16[128,2,32,512]{3,2,1,0:T(8,128)(2,1)}), bf16[128,2,32,512]{3,2,1,0:T(8,128)(2,1)}, u32[]{:S(2)}, u32[]{:S(2)}) async-start(bf16[128,2,32,512]{3,2,1,0:T(8,128)(2,1)} %bitcast.85), calls=%async_computation.1 | async-start | bytes 16777216 | tf_op jit(solution)/shard_map/all_to_all | solution.py:175
  147.5 265.1 %all-to-all-done.1 = bf16[128,2,32,512]{3,2,1,0:T(8,128)(2,1)} async-done(((bf16[128,2,32,512]{3,2,1,0:T(8,128)(2,1)}), bf16[128,2,32,512]{3,2,1,0:T(8,128)(2,1)}, u32[]{:S(2)}, u32[]{:S(2)}) %all-to-all-start.1) | async-done | bytes 8388640 | tf_op jit(solution)/shard_map/all_to_all | solution.py:175
  412.6 107.4 %while.10 = (s32[]{:T(128)}, bf16[16,16,32,256]{3,2,1,0:T(8,128)(2,1)}, bf16[16,16,32,512]{3,2,1,0:T(8,128)(2,1)}, s32[16,16]{1,0:T(8,128)S(1)}, bf16[8,512,256]{2,1,0:T(8,128)(2,1)S(1)}, /*index=5*/s32[]{:T(128)}) while((s32[]{:T(128)}, bf16[16,16,32,256]{3,2,1,0:T(8,128)(2,1)}, bf16[16,16,32,512]{3,2,1,0:T(8,128)(2,1)}, ...), condition=%wide.region_6.7_spmd, body=%wide.region_5.6_spmd.sunk | while | flops 136447120 | bytes 13374893 | solution.py:60
  412.6 2.8 gather_fusion
  415.4 3.9 fusion.50
  419.3 2.8 gather_fusion
  422.1 3.9 fusion.50
  426.0 2.8 gather_fusion
  428.8 3.9 fusion.50
  432.7 2.8 gather_fusion
  435.5 3.9 fusion.50
  439.4 2.8 gather_fusion
  442.2 3.9 fusion.50
  446.1 2.8 gather_fusion
  448.9 3.9 fusion.50
  452.9 2.8 gather_fusion
  455.6 3.9 fusion.50
  459.6 2.8 gather_fusion
  462.3 3.9 fusion.50
  466.3 2.8 gather_fusion
  469.1 3.9 fusion.50
  475.8 3.9 fusion.50
  482.5 3.9 fusion.50
  486.5 2.8 gather_fusion
  489.3 3.9 fusion.50
  493.2 2.8 gather_fusion
  496.0 3.9 fusion.50
  499.9 2.8 gather_fusion
  502.7 3.9 fusion.50
  506.6 2.8 gather_fusion
  509.4 3.9 fusion.50
  513.3 2.8 gather_fusion
  516.1 3.9 fusion.50
  520.0 8.4 %copy.56 = bf16[32,8,32,256]{3,1,2,0:T(8,128)(2,1)} copy(bf16[32,8,32,256]{3,2,1,0:T(8,128)(2,1)} %bitcast.90) | data formatting | bytes 8388608
  528.4 6.4 %copy.51 = bf16[8192,256]{1,0:T(8,128)(2,1)} copy(bf16[8192,256]{0,1:T(8,128)(2,1)} %bitcast.88) | data formatting | bytes 8388608 | tf_op jit(solution)/shard_map/dot_general | solution.py:193
  534.8 3.4 convolution_bitcast_fusion
  (148 shorter events, 48.9 us)
Async XLA Ops:
  0.6 16.4 %copy-start.1 = (f32[4,4,32,384]{3,2,1,0:T(8,128)S(1)}, f32[4,4,32,384]{3,2,1,0:T(8,128)}, u32[]{:S(2)}) copy-start(f32[4,4,32,384]{3,2,1,0:T(8,128)} %param.12) | copy-start | bytes 2359300
  0.6 16.7 %copy-start.4 = (f32[4,32,384]{2,1,0:T(8,128)S(1)}, f32[4,32,384]{2,1,0:T(8,128)}, u32[]{:S(2)}) copy-start(f32[4,32,384]{2,1,0:T(8,128)} %param.14) | copy-start | bytes 589828
  0.7 19.1 %copy-start.6 = (s32[128,1]{0,1:T(1,128)S(1)}, s32[128,1]{0,1:T(1,128)}, u32[]{:S(2)}) copy-start(s32[128,1]{0,1:T(1,128)} %param.19) | copy-start | bytes 1540
  0.7 63.3 %copy-start.7 = (s32[128]{0:T(128)S(1)}, s32[128]{0:T(128)}, u32[]{:S(2)}) copy-start(s32[128]{0:T(128)} %param.18) | copy-start | bytes 1540
  3.0 75.9 %collective-permute-start = (f32[6,4,2,384]{3,2,1,0:T(2,128)S(1)}, f32[6,4,2,384]{3,2,1,0:T(2,128)S(1)}, u32[]{:S(2)}, u32[]{:S(2)}) collective-permute-start(f32[6,4,2,384]{3,2,1,0:T(2,128)S(1)} %get-tuple-element.48), channel_id=1, source_target_pairs={{0,4},{4,8},{8,12},{12,16},{16,20},{20,24},{24,28},{28,32},{32,36}... | collective-permute-start | bytes 221192 | tf_op jit(solution)/shard_map/ppermute | solution.py:16
  7.5 71.4 %collective-permute-start.1 = (f32[6,4,2,384]{3,2,1,0:T(2,128)S(1)}, f32[6,4,2,384]{3,2,1,0:T(2,128)S(1)}, u32[]{:S(2)}, u32[]{:S(2)}) collective-permute-start(f32[6,4,2,384]{3,2,1,0:T(2,128)S(1)} %get-tuple-element.49), channel_id=1, source_target_pairs={{4,0},{8,4},{12,8},{16,12},{20,16},{24,20},{28,24},{32,28},{36,32}... | collective-permute-start | bytes 221192 | tf_op jit(solution)/shard_map/ppermute | solution.py:17
  9.5 69.5 %copy-start.2 = (f32[4,32,384]{2,1,0:T(8,128)S(1)}, f32[4,32,384]{2,1,0:T(8,128)}, u32[]{:S(2)}) copy-start(f32[4,32,384]{2,1,0:T(8,128)} %param.13) | copy-start | bytes 589828
  11.7 69.0 %collective-permute-start.9 = (f32[5,2,32,384]{3,2,1,0:T(8,128)}, f32[5,2,32,384]{3,2,1,0:T(8,128)S(1)}, u32[]{:S(2)}, u32[]{:S(2)}) collective-permute-start(f32[5,2,32,384]{3,2,1,0:T(8,128)} %get-tuple-element.52), channel_id=1, source_target_pairs={{0,1},{1,2},{2,3},{4,5},{5,6},{6,7},{8,9},{9,10},{10,11},{12,13},{... | collective-permute-start | bytes 1474568 | tf_op jit(solution)/shard_map/ppermute | solution.py:16
  14.8 66.0 %collective-permute-start.10 = (f32[5,2,32,384]{3,2,1,0:T(8,128)}, f32[5,2,32,384]{3,2,1,0:T(8,128)S(1)}, u32[]{:S(2)}, u32[]{:S(2)}) collective-permute-start(f32[5,2,32,384]{3,2,1,0:T(8,128)} %get-tuple-element.53), channel_id=1, source_target_pairs={{1,0},{2,1},{3,2},{5,4},{6,5},{7,6},{9,8},{10,9},{11,10},{13,12},{... | collective-permute-start | bytes 1474568 | tf_op jit(solution)/shard_map/ppermute | solution.py:17
  17.5 3.1 collective-permute-start.2
  20.6 22.0 %collective-permute-start.3 = (f32[6,4,32,2]{2,1,3,0:T(4,128)S(1)}, f32[6,4,32,2]{2,1,3,0:T(4,128)S(1)}, u32[]{:S(2)}, u32[]{:S(2)}) collective-permute-start(f32[6,4,32,2]{2,1,3,0:T(4,128)S(1)} %collective-permute-done.2), channel_id=1, source_target_pairs={{0,8},{8,0},{4,12},{12,4},{16,24},{24,16},{20,28},{28,20},{32,40},... | collective-permute-start | bytes 18440 | tf_op jit(solution)/shard_map/ppermute | solution.py:29
  31.3 52.5 %all-to-all-start.2 = ((s32[128,1,2]{2,1,0:T(1,128)}), s32[128,1,2]{2,1,0:T(1,128)S(1)}, u32[]{:S(2)}, u32[]{:S(2)}) async-start(s32[128,1,2]{2,1,0:T(1,128)} %bitcast.27), calls=%async_computation.2 | async-start | bytes 131072 | tf_op jit(solution)/shard_map/all_to_all | solution.py:183
  42.6 5.9 %collective-permute-start.4 = (f32[6,4,32,2]{2,1,3,0:T(4,128)S(1)}, f32[6,4,32,2]{2,1,3,0:T(4,128)S(1)}, u32[]{:S(2)}, u32[]{:S(2)}) collective-permute-start(f32[6,4,32,2]{2,1,3,0:T(4,128)S(1)} %collective-permute-done.3), channel_id=1, source_target_pairs={{0,16},{16,0},{4,20},{20,4},{8,24},{24,8},{12,28},{28,12},{32,48},... | collective-permute-start | bytes 18440 | tf_op jit(solution)/shard_map/ppermute | solution.py:29
  48.5 8.5 %collective-permute-start.5 = (f32[6,4,32,2]{2,1,3,0:T(4,128)S(1)}, f32[6,4,32,2]{2,1,3,0:T(4,128)S(1)}, u32[]{:S(2)}, u32[]{:S(2)}) collective-permute-start(f32[6,4,32,2]{2,1,3,0:T(4,128)S(1)} %collective-permute-done.4), channel_id=1, source_target_pairs={{0,32},{32,0},{4,36},{36,4},{8,40},{40,8},{12,44},{44,12},{16,48},... | collective-permute-start | bytes 18440 | tf_op jit(solution)/shard_map/ppermute | solution.py:29
  57.0 4.6 collective-permute-start.6
  61.6 5.6 %collective-permute-start.7 = (f32[6,4,32,2]{2,1,3,0:T(4,128)S(1)}, f32[6,4,32,2]{2,1,3,0:T(4,128)S(1)}, u32[]{:S(2)}, u32[]{:S(2)}) collective-permute-start(f32[6,4,32,2]{2,1,3,0:T(4,128)S(1)} %collective-permute-done.6), channel_id=1, source_target_pairs={{0,128},{128,0},{4,132},{132,4},{8,136},{136,8},{12,140},{140,12},... | collective-permute-start | bytes 18440 | tf_op jit(solution)/shard_map/ppermute | solution.py:29
  67.1 8.7 %collective-permute-start.8 = (f32[6,4,32,2]{2,1,3,0:T(4,128)S(1)}, f32[6,4,32,2]{2,1,3,0:T(4,128)S(1)}, u32[]{:S(2)}, u32[]{:S(2)}) collective-permute-start(f32[6,4,32,2]{2,1,3,0:T(4,128)S(1)} %collective-permute-done.7), channel_id=1, source_target_pairs={{0,256},{256,0},{4,260},{260,4},{8,264},{264,8},{12,268},{268,12},... | collective-permute-start | bytes 18440 | tf_op jit(solution)/shard_map/ppermute | solution.py:29
  75.8 0.6 copy-start.5
  79.3 1.4 copy-start.3
  83.8 47.0 %all-to-all-start = ((s32[128,1,2]{2,1,0:T(1,128)}), s32[128,1,2]{2,1,0:T(1,128)S(1)}, u32[]{:S(2)}, u32[]{:S(2)}) async-start(s32[128,1,2]{2,1,0:T(1,128)} %bitcast.19), calls=%async_computation | async-start | bytes 131072 | tf_op jit(solution)/shard_map/all_to_all | solution.py:182
  130.8 281.7 %copy-start = (bf16[8,512,256]{2,1,0:T(8,128)(2,1)S(1)}, bf16[8,512,256]{2,1,0:T(8,128)(2,1)}, u32[]{:S(2)}) copy-start(bf16[8,512,256]{2,1,0:T(8,128)(2,1)} %param.17) | copy-start | bytes 6291460
  130.8 281.7 %all-to-all-start.1 = ((bf16[128,2,32,512]{3,2,1,0:T(8,128)(2,1)}), bf16[128,2,32,512]{3,2,1,0:T(8,128)(2,1)}, u32[]{:S(2)}, u32[]{:S(2)}) async-start(bf16[128,2,32,512]{3,2,1,0:T(8,128)(2,1)} %bitcast.85), calls=%async_computation.1 | async-start | bytes 16777216 | tf_op jit(solution)/shard_map/all_to_all | solution.py:175
where the time goes:
time: 541 us; the launch traced here: 540 us
  waiting for transfers between devices  278 us (51%)
  local copies, waits for them, and re-layouts  96.7 us (18%)
  starting transfers between devices  85.4 us (16%)
  matrix products  65.9 us (12%)
  other arithmetic  12.2 us (2%)
    all_to_all x1, waiting for transfers between devices, shards(): lax.all_to_all(raw_blocks.reshape(strips, capacity, row_count, block_size...  265 us
    dot_general x16, matrix products, one_group(): jnp.einsum('erc,ecd->erd', block_group, matrices, preferred_element_type=...  62.5 us
    gather x16, local copies, waits for them, and re-layouts, one_group(): matrices = jnp.take(weights, kind_group, axis=0)  44.4 us
    ppermute x7, starting transfers between devices, partner(): return lax.ppermute(block, axis, route)  28.8 us
    scatter x1, local copies, waits for them, and re-layouts, shards(): raw_blocks = jnp.zeros((slot_count, row_count, block_size), jnp.bfloat16)...  19.7 us
    all_to_all x1, starting transfers between devices, shards(): lax.all_to_all(slot_blocks, 'tile', split_axis=0, concat_axis=0, tiled=True)  19.3 us
    all_to_all x1, starting transfers between devices, shards(): lax.all_to_all(raw_blocks.reshape(strips, capacity, row_count, block_size...  14.3 us
    ppermute x7, waiting for transfers between devices, partner(): return lax.ppermute(block, axis, route)  13.4 us
  transfers between devices with their start and end apart: 14, of which 7 were waited for; matrix products, arithmetic and copies ran while one was open for 8% of the time, Pallas kernels for 0%

commit v1 on v0

--- a/solution.py
+++ b/solution.py
@@ -1,9 +1,257 @@
 import jax
 import jax.numpy as jnp
 from jax import lax
+from jax.experimental import pallas as pl
+from jax.experimental.pallas import tpu as pltpu
 from jax.sharding import PartitionSpec as P
 
+MESH = pl.DeviceIdType.MESH
+RING = 8
 NBD = 16
+GROUP = 16
+BLOCKS = 24
+SB = 512
+DB = 256
+PATTERNS = 8
+SLOTS = 32
+TARGET_ORDER = (4, 3, 5, 2, 6, 1, 7, 0)
+
+
+def remap_kernel(
+    x_ref, w_ref, idx_ref, dst_ref, out0, out1,
+    ag, prod, terms, masks, acc, sib_out, sib_in, rs_out, rs_in,
+    ag_send, ag_recv, sib_send, sib_recv, rs_send, rs_recv,
+):
+    me = lax.axis_index("tile")
+    y, z, c = me // 16, lax.rem(me // 2, 8), lax.rem(me, 2)
+
+    def strip(yy, zz, cc):
+        return yy * 16 + zz * 2 + cc
+
+    along_z = (strip(y, lax.rem(z + 1, RING), c), strip(y, lax.rem(z + RING - 1, RING), c))
+    along_y = (strip(lax.rem(y + 1, RING), z, c), strip(lax.rem(y + RING - 1, RING), z, c))
+    sibling = strip(y, z, 1 - c)
+    gather_to = (along_z, along_y)
+    reduce_to = (along_y, along_z)
+
+    barrier = pltpu.get_barrier_semaphore()
+    for other in (*along_z, *along_y, sibling):
+        pl.semaphore_signal(barrier, inc=1, device_id={"tile": other}, device_id_type=MESH)
+    pl.semaphore_wait(barrier, 5)
+
+    half_rows = BLOCKS // 2
+    streams = [(h, d) for h in range(2) for d in range(2)]
+    started = []
+
+    def gather_copy(h, d, n):
+        k, sub = (n // 2 + 1, n % 2) if n < 6 else (4, d)
+        rows = pl.ds(half_rows * sub, half_rows)
+        src = x_ref.at[h, rows] if k == 1 else ag.at[h, d, k - 2, rows]
+        dst = ag.at[h, 0 if k == 4 else d, k - 1, rows]
+        return pltpu.make_async_remote_copy(
+            src_ref=src, dst_ref=dst, send_sem=ag_send.at[h, d, n], recv_sem=ag_recv.at[h, d, n],
+            device_id={"tile": gather_to[h][d]}, device_id_type=MESH,
+        )
+
+    def start(copy):
+        copy.start()
+        started.append(copy)
+
+    for n in range(2):
+        for h, d in streams:
+            start(gather_copy(h, d, n))
+
+    sub_i = lax.broadcasted_iota(jnp.int32, (NBD * GROUP, SLOTS // 2 * GROUP), 0)
+    lane_i = lax.broadcasted_iota(jnp.int32, (NBD * GROUP, SLOTS // 2 * GROUP), 1)
+    wanted = jnp.where(lax.rem(sub_i, GROUP) == lax.rem(lane_i, GROUP), sub_i // GROUP, -2)
+
+    def one_mask(i, carry):
+        found = dst_ref[pl.ds(i, 1), :] == wanted
+        masks[i] = jnp.where(found, 1.0, 0.0).astype(jnp.bfloat16)
+        return carry
+
+    lax.fori_loop(0, 32, one_mask, 0)
+
+    def multiply(h, j, view):
+        x = view[...].reshape(BLOCKS * GROUP, SB)
+
+        def one_pattern(p, carry):
+            r = jnp.dot(x, w_ref[p], preferred_element_type=jnp.float32)
+            prod[pl.ds(p * BLOCKS, BLOCKS)] = r.astype(jnp.bfloat16).reshape(BLOCKS, GROUP, DB)
+            return carry
+
+        lax.fori_loop(0, PATTERNS, one_pattern, 0)
+
+        def one_target(t, carry):
+            for r in range(2):
+                i = idx_ref[(h * 8 + j) * SLOTS + t * 2 + r]
+                terms[h * 16 + t, pl.ds((j * 2 + r) * GROUP, GROUP), :] = prod[i]
+            return carry
+
+        lax.fori_loop(0, 16, one_target, 0)
+
+    def arrived(h, j):
+        k, d = (j + 1) // 2, (j + 1) % 2
+        multiply(h, j, ag.at[h, 0 if k == 4 else d, k - 1])
+
+    multiply(0, 0, x_ref.at[0])
+    multiply(1, 0, x_ref.at[1])
+    after = {1: [(0, 1), (0, 2)], 2: [(1, 1), (1, 2)], 3: [(0, 3), (0, 4)], 4: [(1, 3), (1, 4)],
+             5: [(0, 5), (0, 6), (1, 5), (1, 6)], 6: [(0, 7), (1, 7)]}
+    for n in range(7):
+        for h, d in streams:
+            gather_copy(h, d, n).wait_recv()
+            if n < 4:
+                start(gather_copy(h, d, n + 2))
+            elif n == 4 + d:
+                start(gather_copy(h, d, 6))
+        for h, j in after.get(n, ()):
+            arrived(h, j)
+
+    def sibling_copy(h, q):
+        return pltpu.make_async_remote_copy(
+            src_ref=sib_out.at[h, q], dst_ref=sib_in.at[h, q], send_sem=sib_send.at[h, q], recv_sem=sib_recv.at[h, q],
+            device_id={"tile": sibling}, device_id_type=MESH,
+        )
+
+    def partial(q):
+        for h in range(2):
+            i = h * 16 + q * 2
+            other = jnp.dot(masks[i + 1], terms[i + 1], preferred_element_type=jnp.float32)
+            sib_out[h, q] = other.astype(jnp.bfloat16)
+            start(sibling_copy(h, q))
+        for h in range(2):
+            i = h * 16 + q * 2
+            acc[h, q] = jnp.dot(masks[i], terms[i], preferred_element_type=jnp.float32)
+
+    def join(q):
+        for h in range(2):
+            sibling_copy(h, q).wait_recv()
+            acc[h, q] += sib_in[h, q].astype(jnp.float32)
+
+    half = NBD * GROUP // 2
+
+    def reduce_copy(h, d, s, part):
+        n = 0 if s == 0 else 1 + 2 * (s - 1) + part
+        rows = pl.ds(part * half, half)
+        return pltpu.make_async_remote_copy(
+            src_ref=rs_out.at[h, d, s, rows], dst_ref=rs_in.at[h, d, s, rows],
+            send_sem=rs_send.at[h, d, n], recv_sem=rs_recv.at[h, d, n],
+            device_id={"tile": reduce_to[h][d]}, device_id_type=MESH,
+        )
+
+    def send_sum(h, d, s, part):
+        q = 4 - s if d == 0 else 4 + s
+        rows = pl.ds(part * half, half)
+        rs_out[h, d, s, rows] = acc[h, q, rows].astype(jnp.bfloat16)
+        start(reduce_copy(h, d, s, part))
+
+    def take_sum(h, d, s, part):
+        q = 3 - s if d == 0 else (5 + s) % 8
+        rows = pl.ds(part * half, half)
+        reduce_copy(h, d, s, part).wait_recv()
+        acc[h, q, rows] += rs_in[h, d, s, rows].astype(jnp.float32)
+
+    for q in (4, 3, 5):
+        partial(q)
+    join(4)
+    for h, d in streams:
+        send_sum(h, d, 0, d)
+    partial(2)
+    partial(6)
+    join(3)
+    join(5)
+    for h, d in streams:
+        send_sum(h, d, 1, 1 - d)
+    for h, d in streams:
+        take_sum(h, d, 0, d)
+        send_sum(h, d, 1, d)
+    for q in (1, 7, 0):
+        partial(q)
+    for q in (2, 6, 1, 7, 0):
+        join(q)
+    for s in (1, 2):
+        for part in range(2):
+            for h, d in streams:
+                side = (1 - d, d)[part]
+                take_sum(h, d, s, side)
+                send_sum(h, d, s + 1, side)
+    for part in range(2):
+        for h, d in streams:
+            take_sum(h, d, 3, (1 - d, d)[part])
+    for h, out in ((0, out0), (1, out1)):
+        for b in range(NBD):
+            out[:, b * DB : (b + 1) * DB] = acc[h, 0, b * GROUP : (b + 1) * GROUP, :]
+    for copy in started:
+        copy.wait_send()
+
+
+def remap(x, weights, idx, dst):
+    vmem = pl.BlockSpec(memory_space=pltpu.VMEM)
+    smem = pl.BlockSpec(memory_space=pltpu.SMEM)
+    rows = NBD * GROUP
+    bf16, f32 = jnp.bfloat16, jnp.float32
+    return pl.pallas_call(
+        remap_kernel,
+        out_shape=[jax.ShapeDtypeStruct((GROUP, NBD * DB), f32)] * 2,
+        in_specs=[vmem, vmem, smem, vmem],
+        out_specs=[vmem, vmem],
+        scratch_shapes=[
+            pltpu.VMEM((2, 2, 4, BLOCKS, GROUP, SB), bf16),
+            pltpu.VMEM((PATTERNS * BLOCKS, GROUP, DB), bf16),
+            pltpu.VMEM((32, rows, DB), bf16),
+            pltpu.VMEM((32, rows, DB), bf16),
+            pltpu.VMEM((2, RING, rows, DB), f32),
+            pltpu.VMEM((2, RING, rows, DB), bf16),
+            pltpu.VMEM((2, RING, rows, DB), bf16),
+            pltpu.VMEM((2, 2, 4, rows, DB), bf16),
+            pltpu.VMEM((2, 2, 4, rows, DB), bf16),
+            pltpu.SemaphoreType.DMA((2, 2, 7)),
+            pltpu.SemaphoreType.DMA((2, 2, 7)),
+            pltpu.SemaphoreType.DMA((2, RING)),
+            pltpu.SemaphoreType.DMA((2, RING)),
+            pltpu.SemaphoreType.DMA((2, 2, 7)),
+            pltpu.SemaphoreType.DMA((2, 2, 7)),
+        ],
+        compiler_params=pltpu.CompilerParams(
+            collective_id=1, has_side_effects=True, vmem_limit_bytes=52 * 1024 * 1024
+        ),
+        cost_estimate=pl.CostEstimate(flops=13_000_000_000, bytes_accessed=4_000_000, transcendentals=0),
+    )(x, weights, idx, dst)
+
+
+def slot_tables(src_block, dst_tile, dst_block, pattern):
+    targets = dst_tile[:, 0]
+    entries = targets.shape[0]
+    order = jnp.arange(entries, dtype=jnp.int32)
+    same = (targets[:, None] == targets[None, :]) & (order[None, :] < order[:, None])
+    slot = targets * 2 + jnp.sum(same.astype(jnp.int32), 1)
+    hit = slot[:, None] == jnp.arange(2 * lax.axis_size("tile"), dtype=jnp.int32)[None, :]
+    values = jnp.stack([src_block, pattern, dst_block]) + 1
+    return jnp.sum(jnp.where(hit[None], values[:, :, None], 0), 1) - 1
+
+
+def local_tables(gathered):
+    me = lax.axis_index("tile")
+    y, z, c = me // 16, (me // 2) % 8, me % 2
+    full = gathered.reshape(8, 8, 2, 3, 8, 8, 2, 2)
+    full = lax.dynamic_index_in_dim(full, c, 2, keepdims=False)
+    by_z = lax.dynamic_index_in_dim(full, y, 0, keepdims=False)
+    by_z = lax.dynamic_index_in_dim(by_z, z, 3, keepdims=False)
+    by_y = lax.dynamic_index_in_dim(full, z, 1, keepdims=False)
+    by_y = lax.dynamic_index_in_dim(by_y, y, 2, keepdims=False)
+
+    def turned(table, source, target):
+        table = lax.dynamic_slice_in_dim(jnp.concatenate([table, table], 0), source, 8, 0)
+        table = table[jnp.array([0, 7, 1, 6, 2, 5, 3, 4])]
+        table = lax.dynamic_slice_in_dim(jnp.concatenate([table, table], 2), target, 8, 2)
+        return jnp.where(c == 0, table, table[:, :, :, ::-1])
+
+    both = jnp.stack([turned(by_z, z, y), turned(by_y, y, z)])
+    src, pat, dst = both[:, :, 0], both[:, :, 1], both[:, :, 2]
+    idx = jnp.maximum(pat * BLOCKS + src, 0).reshape(-1)
+    dst = dst.transpose(0, 2, 3, 1, 4).reshape(32, 16)
+    return idx, jnp.repeat(dst, GROUP, 1)
 
 
 def padded(shard, sides, width, wrap):
@@ -19,16 +267,6 @@
     return shard
 
 
-def partner(block, axis, stride):
-    count = lax.axis_size(axis)
-    route = []
-    for low in range(count):
-        high = low | 1 << stride
-        if high != low and high < count:
-            route += [(low, high), (high, low)]
-    return lax.ppermute(block, axis, route)
-
-
 def minmod(first, second):
     return jnp.where(
         first * second > 0.0, jnp.sign(first) * jnp.minimum(jnp.abs(first), jnp.abs(second)), 0.0
@@ -41,24 +279,6 @@
     upwind = jnp.maximum(courant, 0.0) * (left_cell + 0.5 * (1.0 - courant) * left_slope)
     downwind = jnp.minimum(courant, 0.0) * (right_cell - 0.5 * (1.0 + courant) * right_slope)
     return opening * (upwind + downwind)
-
-
-def apply_weights(blocks, kind_ids, weights):
-    group_size = 16
-    entry_count = blocks.shape[0]
-    grouped = blocks.reshape((entry_count // group_size, group_size) + blocks.shape[1:])
-    kind_groups = kind_ids.reshape(entry_count // group_size, group_size)
-
-    def one_group(members):
-        block_group, kind_group = members
-        matrices = jnp.take(weights, kind_group, axis=0)
-        products = jnp.einsum(
-            "erc,ecd->erd", block_group, matrices, preferred_element_type=jnp.float32
-        )
-        return products.astype(jnp.bfloat16)
-
-    result = lax.map(one_group, (grouped, kind_groups))
-    return result.reshape((entry_count,) + result.shape[2:])
 
 
 def shards(
@@ -99,9 +319,8 @@
         ],
         0,
     )
-    partner_rows = top_rows
-    for bit_number in range(lax.axis_size("tile").bit_length() - 1):
-        partner_rows = partner(partner_rows, "tile", bit_number)
+    strips = lax.axis_size("tile")
+    partner_rows = lax.ppermute(top_rows, "tile", [(i, strips - 1 - i) for i in range(strips)])
     mirrored = jnp.flip(partner_rows, (2, 3))
     ghost_cells = mirrored[:tracer_count]
     ghost_ocean = mirrored[tracer_count, 0, :, 0]
@@ -143,59 +362,12 @@
     divergence = east_flux - west_flux + (north_flux - south_flux) + (below_flux - above_flux)
     new_tracers = tracers - divergence
     payload = jnp.stack([new_tracers, divergence]).astype(jnp.bfloat16)
-    row_count = 2 * tracer_count * levels_dev
-    block_size = weights.shape[1]
-    source_blocks = payload.reshape(
-        row_count, columns * rows_dev // block_size, block_size
-    ).transpose(1, 0, 2)
-    strips = lax.axis_size("tile")
-    capacity = max(2, 2 * src_block.shape[0] // strips)
-    slot_count = strips * capacity
-    targets = dst_tile[:, 0]
-    owner_hits = (targets[:, None] == jnp.arange(strips, dtype=jnp.int32)[None, :]).astype(
-        jnp.int32
-    )
-    slot_ranks = jnp.sum(jnp.cumsum(owner_hits, 0) * owner_hits, 1) - 1
-    slot_index = targets * capacity + slot_ranks
-    slot_blocks = (
-        jnp.full((slot_count,), -1, jnp.int32)
-        .at[slot_index]
-        .set(dst_block)
-        .reshape(strips, capacity)
-    )
-    raw_blocks = (
-        jnp.zeros((slot_count, row_count, block_size), jnp.bfloat16)
-        .at[slot_index]
-        .set(source_blocks[src_block])
-    )
-    slot_kinds = (
-        jnp.zeros((slot_count,), jnp.int32).at[slot_index].set(pattern).reshape(strips, capacity)
-    )
-    arrived, arrived_blocks, arrived_kinds = (
-        lax.all_to_all(
-            raw_blocks.reshape(strips, capacity, row_count, block_size),
-            "tile",
-            split_axis=0,
-            concat_axis=0,
-            tiled=True,
-        ),
-        lax.all_to_all(slot_blocks, "tile", split_axis=0, concat_axis=0, tiled=True),
-        lax.all_to_all(slot_kinds, "tile", split_axis=0, concat_axis=0, tiled=True),
-    )
-    slot_terms = apply_weights(
-        arrived.reshape(slot_count, row_count, block_size),
-        arrived_kinds.reshape(slot_count),
-        weights,
-    )
-    block_hits = (
-        arrived_blocks.reshape(slot_count)[None, :] == jnp.arange(NBD, dtype=jnp.int32)[:, None]
-    ).astype(jnp.bfloat16)
-    summed = jnp.dot(
-        block_hits, slot_terms.reshape(slot_count, -1), preferred_element_type=jnp.float32
-    )
-    shaped = summed.reshape(NBD, 2, tracer_count, levels_dev, -1).transpose(1, 2, 3, 0, 4)
-    shaped = shaped.reshape(2, tracer_count, levels_dev, -1)
-    return (new_tracers, shaped[0], shaped[1])
+    blocks = payload.reshape(2, GROUP, BLOCKS, SB).transpose(0, 2, 1, 3)
+    gathered = lax.all_gather(slot_tables(src_block, dst_tile, dst_block, pattern), "tile")
+    idx, dst = local_tables(gathered)
+    fields, fluxes = remap(blocks, weights, idx, dst)
+    shape = (tracer_count, levels_dev, NBD * DB)
+    return (new_tracers, fields.reshape(shape), fluxes.reshape(shape))
 
 
 def solution(mesh):

time: 541 us -> 193 us (0.36)
  the two profiles are of different devices: /device:TPU:107 before, /device:TPU:1 now
where the time goes in v1:
time: 193 us; the launch traced here: 192 us
  Pallas kernels  66.4 us (34%)
  blocking collectives  48.2 us (25%)
  local copies, waits for them, and re-layouts  39.5 us (20%)
  starting transfers between devices  25.4 us (13%)
  other arithmetic  10.8 us (6%)
    pallas_call x1, Pallas kernels, remap(): pl.pallas_call(remap_kernel, out_shape=[jax.ShapeDtypeStruct((GROUP, NBD...  66.4 us
    all_gather x1, blocking collectives, shards(): lax.all_gather(slot_tables(src_block, dst_tile, dst_block, pattern), 'tile')  48.2 us
    reshape x1, local copies, waits for them, and re-layouts, local_tables(): full = gathered.reshape(8, 8, 2, 3, 8, 8, 2, 2)  26.7 us
    ppermute x1, starting transfers between devices, shards(): lax.ppermute(top_rows, 'tile', [(i, strips - 1 - i) for i in range(strips)])  11.9 us
    ppermute x2, starting transfers between devices, padded(): before = lax.ppermute(last, axis, up)  6.82 us
    ppermute x2, starting transfers between devices, padded(): after = lax.ppermute(leading, axis, down)  6.61 us
  transfers between devices with their start and end apart: 5, of which 0 were waited for; matrix products, arithmetic and copies ran while one was open for 21% of the time, Pallas kernels for 0%

profile of v1, /device:TPU:1, one launch (start us, length us, event | category | flops | bytes accessed | tf_op | source)
XLA Modules:
  0.0 191.5 jit_solution(5381480914926426310)
XLA Ops:
  0.7 1.0 copy.88
  1.8 1.5 pad_maximum_fusion.12
  3.3 5.5 %collective-permute-start = (f32[6,4,2,384]{3,2,1,0:T(2,128)}, f32[6,4,2,384]{3,2,1,0:T(2,128)S(1)}, u32[]{:S(2)}, u32[]{:S(2)}) collective-permute-start(f32[6,4,2,384]{3,2,1,0:T(2,128)} %get-tuple-element.14), channel_id=1, source_target_pairs={{0,4},{4,8},{8,12},{12,16},{16,20},{20,24},{24,28},{28,32},{32,36}... | collective-permute-start | bytes 221192 | tf_op jit(solution)/shard_map/ppermute | solution.py:264
  8.9 5.3 %collective-permute-start.1 = (f32[6,4,2,384]{3,2,1,0:T(2,128)S(1)}, f32[6,4,2,384]{3,2,1,0:T(2,128)S(1)}, u32[]{:S(2)}, u32[]{:S(2)}) collective-permute-start(f32[6,4,2,384]{3,2,1,0:T(2,128)S(1)} %get-tuple-element.15), channel_id=1, source_target_pairs={{4,0},{8,4},{12,8},{16,12},{20,16},{24,20},{28,24},{32,28},{36,32}... | collective-permute-start | bytes 221192 | tf_op jit(solution)/shard_map/ppermute | solution.py:265
  14.2 1.1 fusion.9
  15.3 1.3 collective-permute-start.3
  16.6 1.3 collective-permute-start.4
  17.9 0.1 slice.174
  18.1 0.2 copy.110
  18.3 0.1 copy.111
  18.5 11.9 %collective-permute-start.2 = (f32[6,4,32,2]{2,0,3,1:T(8,128)S(1)}, f32[6,4,32,2]{2,0,3,1:T(8,128)S(1)}, u32[]{:S(2)}, u32[]{:S(2)}) collective-permute-start(f32[6,4,32,2]{2,0,3,1:T(8,128)S(1)} %pad_maximum_fusion.14), channel_id=1, source_target_pairs={{0,508},{4,504},{8,500},{12,496},{16,492},{20,488},{24,484},{28,48... | collective-permute-start | bytes 18440 | tf_op jit(solution)/shard_map/ppermute | solution.py:323
  30.5 0.2 convert_reduce_fusion
  30.8 0.1 select_reduce_fusion
  30.9 48.2 %all-gather.1 = s32[128,3,256]{2,1,0:T(4,128)S(1)} all-gather(s32[1,3,256]{2,1,0:T(4,128)S(1)} %add_bitcast_fusion), channel_id=2, replica_groups=mesh['tile'=128,'lev'=4] {'tile'}, dimensions={0}, use_global_device_ids=true | all-gather | bytes 396288 | tf_op jit(solution)/shard_map/all_gather | solution.py:366
  79.2 0.2 copy.100
  79.4 26.7 %reshape.184 = s32[8,8,2,3,8,8,2,2]{2,1,0,7,6,5,4,3:T(8,128)} reshape(s32[128,3,256]{0,2,1:T(8,128)S(1)} %copy.100) | data formatting | bytes 786432 | tf_op jit(solution)/shard_map/reshape | solution.py:237
  106.1 2.8 %constant_dynamic-slice_fusion = s32[8,1,1,3,1,8,2,2]{2,1,0,7,6,5,4,3:T(1,128)S(1)} fusion(s32[8,8,2,3,8,8,2,2]{2,1,0,7,6,5,4,3:T(8,128)} %reshape.184, s32[]{:T(128)S(6)} %select_n.108, s32[]{:T(128)S(6)} %select_n.104, s32[]{:T(128)S(6)} %select_n.102), kind=kLoop, calls=%fused_computation.97 | loop fusion | bytes 6156 | tf_op jit(solution)/shard_map/jit(dynamic_index_in_dim)/dynamic_slice | solution.py:242
  108.9 1.2 constant_dynamic-slice_fusion.1
  110.1 0.8 copy.104
  111.0 0.6 gather_fusion.1
  111.7 0.7 copy.101
  112.3 0.1 dynamic-slice_add_fusion
  112.5 0.6 gather_fusion
  113.2 0.1 dynamic-slice_add_fusion.1
  113.5 0.3 copy.108
  113.8 0.1 reshape.185
  114.0 0.3 copy.107
  114.2 0.2 max.29.idx_ref
  114.4 0.1 copy.92
  114.5 0.1 copy.112
  114.6 0.1 slice.178
  114.8 0.1 slice.182
  114.9 0.1 copy.95
  115.1 0.1 slice.185
  115.2 0.2 copy.96
  115.5 1.2 add_multiply_fusion.2
  116.8 0.2 maximum_maximum_fusion
  117.1 1.3 add_multiply_fusion.1
  118.6 1.4 maximum_maximum_fusion.1
  120.0 1.2 add_multiply_fusion
  121.2 1.4 fusion.24
  122.6 0.3 stack.30
  122.9 0.1 copy.98
  123.1 0.3 stack.31
  123.4 0.1 copy.99
  123.6 66.4 %shard_map.139 = (f32[16,4096]{1,0:T(8,128)S(1)}, f32[16,4096]{1,0:T(8,128)S(1)}) custom-call(bf16[2,24,16,512]{3,2,1,0:T(8,128)(2,1)S(1)} %maximum_bitcast_fusion.x_ref, bf16[8,512,256]{2,1,0:T(8,128)(2,1)} %w_ref.1, s32[512]{0:T(512)S(1)} %max.29.idx_ref, s32[32,256]{1,0:T(8,128)S(1)} %copy.109.dst_ref), custom_call_target="tpu_custom_call" | custom-call | flops 12999999488 | bytes 4000000 | tf_op jit(solution)/shard_map/pallas_call | solution.py:194
  190.0 0.8 reshape.187
  190.7 0.8 reshape.188
  (61 shorter events, 1.5 us)
Async XLA Ops:
  0.6 1.2 copy-start
  0.6 13.5 %copy-start.2 = (f32[4,32,384]{2,1,0:T(8,128)S(1)}, f32[4,32,384]{2,1,0:T(8,128)}, u32[]{:S(2)}) copy-start(f32[4,32,384]{2,1,0:T(8,128)} %param.15) | copy-start | bytes 589828
  3.3 14.9 %copy-start.3 = (f32[4,32,384]{2,1,0:T(8,128)S(1)}, f32[4,32,384]{2,1,0:T(8,128)}, u32[]{:S(2)}) copy-start(f32[4,32,384]{2,1,0:T(8,128)} %param.14) | copy-start | bytes 589828
  3.3 113.4 %collective-permute-start = (f32[6,4,2,384]{3,2,1,0:T(2,128)}, f32[6,4,2,384]{3,2,1,0:T(2,128)S(1)}, u32[]{:S(2)}, u32[]{:S(2)}) collective-permute-start(f32[6,4,2,384]{3,2,1,0:T(2,128)} %get-tuple-element.14), channel_id=1, source_target_pairs={{0,4},{4,8},{8,12},{12,16},{16,20},{20,24},{24,28},{28,32},{32,36}... | collective-permute-start | bytes 221192 | tf_op jit(solution)/shard_map/ppermute | solution.py:264
  8.9 107.8 %collective-permute-start.1 = (f32[6,4,2,384]{3,2,1,0:T(2,128)S(1)}, f32[6,4,2,384]{3,2,1,0:T(2,128)S(1)}, u32[]{:S(2)}, u32[]{:S(2)}) collective-permute-start(f32[6,4,2,384]{3,2,1,0:T(2,128)S(1)} %get-tuple-element.15), channel_id=1, source_target_pairs={{4,0},{8,4},{12,8},{16,12},{20,16},{24,20},{28,24},{32,28},{36,32}... | collective-permute-start | bytes 221192 | tf_op jit(solution)/shard_map/ppermute | solution.py:265
  14.2 16.3 %copy-start.8 = (s32[128,1]{0,1:T(1,128)S(1)}, s32[128,1]{0,1:T(1,128)}, u32[]{:S(2)}) copy-start(s32[128,1]{0,1:T(1,128)} %param.19) | copy-start | bytes 1540
  14.2 16.6 %copy-start.4 = (s32[128]{0:T(128)S(1)}, s32[128]{0:T(128)}, u32[]{:S(2)}) copy-start(s32[128]{0:T(128)} %param.20) | copy-start | bytes 1540
  14.2 16.6 %copy-start.5 = (s32[128]{0:T(128)S(1)}, s32[128]{0:T(128)}, u32[]{:S(2)}) copy-start(s32[128]{0:T(128)} %param.21) | copy-start | bytes 1540
  14.2 16.5 %copy-start.6 = (s32[128]{0:T(128)S(1)}, s32[128]{0:T(128)}, u32[]{:S(2)}) copy-start(s32[128]{0:T(128)} %param.18) | copy-start | bytes 1540
  15.3 103.2 %collective-permute-start.3 = (f32[5,2,32,384]{3,2,1,0:T(8,128)}, f32[5,2,32,384]{3,2,1,0:T(8,128)S(1)}, u32[]{:S(2)}, u32[]{:S(2)}) collective-permute-start(f32[5,2,32,384]{3,2,1,0:T(8,128)} %get-tuple-element.18), channel_id=1, source_target_pairs={{0,1},{1,2},{2,3},{4,5},{5,6},{6,7},{8,9},{9,10},{10,11},{12,13},{... | collective-permute-start | bytes 1474568 | tf_op jit(solution)/shard_map/ppermute | solution.py:264
  16.6 102.0 %collective-permute-start.4 = (f32[5,2,32,384]{3,2,1,0:T(8,128)}, f32[5,2,32,384]{3,2,1,0:T(8,128)}, u32[]{:S(2)}, u32[]{:S(2)}) collective-permute-start(f32[5,2,32,384]{3,2,1,0:T(8,128)} %get-tuple-element.19), channel_id=1, source_target_pairs={{1,0},{2,1},{3,2},{5,4},{6,5},{7,6},{9,8},{10,9},{11,10},{13,12},{... | collective-permute-start | bytes 1474568 | tf_op jit(solution)/shard_map/ppermute | solution.py:265
  18.5 96.2 %collective-permute-start.2 = (f32[6,4,32,2]{2,0,3,1:T(8,128)S(1)}, f32[6,4,32,2]{2,0,3,1:T(8,128)S(1)}, u32[]{:S(2)}, u32[]{:S(2)}) collective-permute-start(f32[6,4,32,2]{2,0,3,1:T(8,128)S(1)} %pad_maximum_fusion.14), channel_id=1, source_target_pairs={{0,508},{4,504},{8,500},{12,496},{16,492},{20,488},{24,484},{28,48... | collective-permute-start | bytes 18440 | tf_op jit(solution)/shard_map/ppermute | solution.py:323
  106.1 4.8 %copy-start.7 = (s32[8]{0:T(128)S(1)}, s32[8]{0:T(128)}, u32[]{:S(2)}) copy-start(s32[8]{0:T(128)} %constant.275) | copy-start | bytes 100
  115.5 1.2 copy-start.1

commit v2 on v1

v2 whole, which is shorter than its diff:
```python
import jax
import jax.numpy as jnp
from jax import lax
from jax.experimental import pallas as pl
from jax.experimental.pallas import tpu as pltpu
from jax.sharding import PartitionSpec as P

MESH = pl.DeviceIdType.MESH
RING = 8
NBD = 16
GROUP = 16
BLOCKS = 24
SB = 512
DB = 256
PATTERNS = 8
SLOTS = 32
TARGET_ORDER = (4, 3, 5, 2, 6, 1, 7, 0)


def remap_kernel(
    x_ref, w_ref, tab_ref, out0, out1,
    ag, prod, terms, masks, acc, sib_out, sib_in, rs_out, rs_in,
    ag_send, ag_recv, sib_send, sib_recv, rs_send, rs_recv,
):
    me = lax.axis_index("tile")
    y, z, c = me // 16, lax.rem(me // 2, 8), lax.rem(me, 2)

    def strip(yy, zz, cc):
        return yy * 16 + zz * 2 + cc

    along_z = (strip(y, lax.rem(z + 1, RING), c), strip(y, lax.rem(z + RING - 1, RING), c))
    along_y = (strip(lax.rem(y + 1, RING), z, c), strip(lax.rem(y + RING - 1, RING), z, c))
    sibling = strip(y, z, 1 - c)
    gather_to = (along_z, along_y)
    reduce_to = (along_y, along_z)

    barrier = pltpu.get_barrier_semaphore()
    for other in (*along_z, *along_y, sibling):
        pl.semaphore_signal(barrier, inc=1, device_id={"tile": other}, device_id_type=MESH)
    pl.semaphore_wait(barrier, 5)

    half_rows = BLOCKS // 2
    streams = [(h, d) for h in range(2) for d in range(2)]
    started = []

    def gather_copy(h, d, n):
        k, sub = (n // 2 + 1, n % 2) if n < 6 else (4, d)
        rows = pl.ds(half_rows * sub, half_rows)
        src = x_ref.at[h, rows] if k == 1 else ag.at[h, d, k - 2, rows]
        dst = ag.at[h, 0 if k == 4 else d, k - 1, rows]
        return pltpu.make_async_remote_copy(
            src_ref=src, dst_ref=dst, send_sem=ag_send.at[h, d, n], recv_sem=ag_recv.at[h, d, n],
            device_id={"tile": gather_to[h][d]}, device_id_type=MESH,
        )

    def start(copy):
        copy.start()
        started.append(copy)

    for n in range(2):
        for h, d in streams:
            start(gather_copy(h, d, n))

    sub_i = lax.broadcasted_iota(jnp.int32, (NBD * GROUP, SLOTS // 2 * GROUP), 0)
    lane_i = lax.broadcasted_iota(jnp.int32, (NBD * GROUP, SLOTS // 2 * GROUP), 1)
    wanted = jnp.where(lax.rem(sub_i, GROUP) == lax.rem(lane_i, GROUP), sub_i // GROUP, -2)
    slot_of_lane = lax.broadcasted_iota(jnp.int32, (1, SLOTS // 2 * GROUP), 1) // GROUP

    def one_mask(i, carry):
        h, t = i // 16, lax.rem(i, 16)
        blocks = jnp.full((1, SLOTS // 2 * GROUP), -1, jnp.int32)
        for j in range(8):
            for r in range(2):
                blocks = jnp.where(slot_of_lane == j * 2 + r, tab_ref[h * 8 + j, 2 * SLOTS + t * 2 + r], blocks)
        masks[i] = jnp.where(blocks == wanted, 1.0, 0.0).astype(jnp.bfloat16)
        return carry

    lax.fori_loop(0, 32, one_mask, 0)

    def multiply(h, j, view):
        x = view[...].reshape(BLOCKS * GROUP, SB)

        def one_pattern(p, carry):
            r = jnp.dot(x, w_ref[p], preferred_element_type=jnp.float32)
            prod[pl.ds(p * BLOCKS, BLOCKS)] = r.astype(jnp.bfloat16).reshape(BLOCKS, GROUP, DB)
            return carry

        lax.fori_loop(0, PATTERNS, one_pattern, 0)

        def one_target(t, carry):
            for r in range(2):
                src, pat = tab_ref[h * 8 + j, t * 2 + r], tab_ref[h * 8 + j, SLOTS + t * 2 + r]
                i = jnp.clip(pat * BLOCKS + src, 0, PATTERNS * BLOCKS - 1)
                terms[h * 16 + t, pl.ds((j * 2 + r) * GROUP, GROUP), :] = prod[i]
            return carry

        lax.fori_loop(0, 16, one_target, 0)

    def arrived(h, j):
        k, d = (j + 1) // 2, (j + 1) % 2
        multiply(h, j, ag.at[h, 0 if k == 4 else d, k - 1])

    multiply(0, 0, x_ref.at[0])
    multiply(1, 0, x_ref.at[1])
    after = {1: [(0, 1), (0, 2)], 2: [(1, 1), (1, 2)], 3: [(0, 3), (0, 4)], 4: [(1, 3), (1, 4)],
             5: [(0, 5), (0, 6), (1, 5), (1, 6)], 6: [(0, 7), (1, 7)]}
    for n in range(7):
        for h, d in streams:
            gather_copy(h, d, n).wait_recv()
            if n < 4:
                start(gather_copy(h, d, n + 2))
            elif n == 4 + d:
                start(gather_copy(h, d, 6))
        for h, j in after.get(n, ()):
            arrived(h, j)

    def sibling_copy(h, q):
        return pltpu.make_async_remote_copy(
            src_ref=sib_out.at[h, q], dst_ref=sib_in.at[h, q], send_sem=sib_send.at[h, q], recv_sem=sib_recv.at[h, q],
            device_id={"tile": sibling}, device_id_type=MESH,
        )

    def partial(q):
        for h in range(2):
            i = h * 16 + q * 2
            other = jnp.dot(masks[i + 1], terms[i + 1], preferred_element_type=jnp.float32)
            sib_out[h, q] = other.astype(jnp.bfloat16)
            start(sibling_copy(h, q))
        for h in range(2):
            i = h * 16 + q * 2
            acc[h, q] = jnp.dot(masks[i], terms[i], preferred_element_type=jnp.float32)

    def join(q):
        for h in range(2):
            sibling_copy(h, q).wait_recv()
            acc[h, q] += sib_in[h, q].astype(jnp.float32)

    half = NBD * GROUP // 2

    def reduce_copy(h, d, s, part):
        n = 0 if s == 0 else 1 + 2 * (s - 1) + part
        rows = pl.ds(part * half, half)
        return pltpu.make_async_remote_copy(
            src_ref=rs_out.at[h, d, s, rows], dst_ref=rs_in.at[h, d, s, rows],
            send_sem=rs_send.at[h, d, n], recv_sem=rs_recv.at[h, d, n],
            device_id={"tile": reduce_to[h][d]}, device_id_type=MESH,
        )

    def send_sum(h, d, s, part):
        q = 4 - s if d == 0 else 4 + s
        rows = pl.ds(part * half, half)
        rs_out[h, d, s, rows] = acc[h, q, rows].astype(jnp.bfloat16)
        start(reduce_copy(h, d, s, part))

    def take_sum(h, d, s, part):
        q = 3 - s if d == 0 else (5 + s) % 8
        rows = pl.ds(part * half, half)
        reduce_copy(h, d, s, part).wait_recv()
        acc[h, q, rows] += rs_in[h, d, s, rows].astype(jnp.float32)

    for q in (4, 3, 5):
        partial(q)
    join(4)
    for h, d in streams:
        send_sum(h, d, 0, d)
    partial(2)
    partial(6)
    join(3)
    join(5)
    for h, d in streams:
        send_sum(h, d, 1, 1 - d)
    for h, d in streams:
        take_sum(h, d, 0, d)
        send_sum(h, d, 1, d)
    for q in (1, 7, 0):
        partial(q)
    for q in (2, 6, 1, 7, 0):
        join(q)
    for s in (1, 2):
        for part in range(2):
            for h, d in streams:
                side = (1 - d, d)[part]
                take_sum(h, d, s, side)
                send_sum(h, d, s + 1, side)
    for part in range(2):
        for h, d in streams:
            take_sum(h, d, 3, (1 - d, d)[part])
    for h, out in ((0, out0), (1, out1)):
        for b in range(NBD):
            out[:, b * DB : (b + 1) * DB] = acc[h, 0, b * GROUP : (b + 1) * GROUP, :]
    for copy in started:
        copy.wait_send()


def remap(x, weights, table):
    vmem = pl.BlockSpec(memory_space=pltpu.VMEM)
    smem = pl.BlockSpec(memory_space=pltpu.SMEM)
    rows = NBD * GROUP
    bf16, f32 = jnp.bfloat16, jnp.float32
    return pl.pallas_call(
        remap_kernel,
        out_shape=[jax.ShapeDtypeStruct((GROUP, NBD * DB), f32)] * 2,
        in_specs=[vmem, vmem, smem],
        out_specs=[vmem, vmem],
        scratch_shapes=[
            pltpu.VMEM((2, 2, 4, BLOCKS, GROUP, SB), bf16),
            pltpu.VMEM((PATTERNS * BLOCKS, GROUP, DB), bf16),
            pltpu.VMEM((32, rows, DB), bf16),
            pltpu.VMEM((32, rows, DB), bf16),
            pltpu.VMEM((2, RING, rows, DB), f32),
            pltpu.VMEM((2, RING, rows, DB), bf16),
            pltpu.VMEM((2, RING, rows, DB), bf16),
            pltpu.VMEM((2, 2, 4, rows, DB), bf16),
            pltpu.VMEM((2, 2, 4, rows, DB), bf16),
            pltpu.SemaphoreType.DMA((2, 2, 7)),
            pltpu.SemaphoreType.DMA((2, 2, 7)),
            pltpu.SemaphoreType.DMA((2, RING)),
            pltpu.SemaphoreType.DMA((2, RING)),
            pltpu.SemaphoreType.DMA((2, 2, 7)),
            pltpu.SemaphoreType.DMA((2, 2, 7)),
        ],
        compiler_params=pltpu.CompilerParams(
            collective_id=1, has_side_effects=True, vmem_limit_bytes=52 * 1024 * 1024
        ),
        cost_estimate=pl.CostEstimate(flops=13_000_000_000, bytes_accessed=4_000_000, transcendentals=0),
    )(x, weights, table)


def minmod(first, second):
    return jnp.maximum(jnp.minimum(first, second), jnp.minimum(jnp.maximum(first, second), 0.0))


def coefficients(courant, opening):
    up, down = jnp.maximum(courant, 0.0) * opening, jnp.minimum(courant, 0.0) * opening
    return up, up * (0.5 * (1.0 - courant)), down, down * (0.5 * (1.0 + courant))


def flux(coefs, left, left_slope, right, right_slope):
    up, up_slope, down, down_slope = coefs
    return (up * left + up_slope * left_slope) + (down * right - down_slope * right_slope)


NEAR = {1: 1, 2: 3, 3: 5, 4: 7, 5: 6, 6: 4, 7: 2}


def advect_kernel(
    tr, u_ref, v_ref, w_ref, land_ref, tab_ref, new_ref, x_ref, tab_out,
    up_out, down_out, up_in, down_in, w_in, west_tr, east_tr, west_u, west_land, east_land,
    fold_out, fold_in, mirrored, tab_in, div, staged, send, recv,
):
    tiles, levs = lax.axis_size("tile"), lax.axis_size("lev")
    me, lev = lax.axis_index("tile"), lax.axis_index("lev")
    y, z, c = me // 16, lax.rem(me // 2, 8), lax.rem(me, 2)
    ntr, nlev, cols, rows = tr.shape
    east, west = {"tile": lax.rem(me + 1, tiles)}, {"tile": lax.rem(me + tiles - 1, tiles)}
    fold = {"tile": tiles - 1 - me}
    below, above = {"lev": lax.rem(lev + 1, levs)}, {"lev": lax.rem(lev + levs - 1, levs)}
    table_to = []
    for o in range(1, 8):
        zz, yy = lax.rem(z + o, 8), lax.rem(y + o, 8)
        table_to.append((o, 0, zz, {"tile": y * 16 + zz * 2 + c}))
        table_to.append((o, 1, yy, {"tile": yy * 16 + z * 2 + c}))
    partners = [east, west, fold, below, above] + [entry[3] for entry in table_to]
    barrier = pltpu.get_barrier_semaphore()
    for other in partners:
        pl.semaphore_signal(barrier, inc=1, device_id=other, device_id_type=MESH)
    down_out[...] = tr[:, 0:2].astype(jnp.bfloat16)
    up_out[...] = tr[:, nlev - 2 : nlev].astype(jnp.bfloat16)
    lane = lax.broadcasted_iota(jnp.int32, (cols, 128), 1)
    top = rows - 128
    packed = jnp.zeros((cols, 128), jnp.float32)
    for q in range(ntr * nlev):
        tile = tr[q // nlev, q % nlev, :, top:]
        packed = jnp.where(lane == 2 * q, pltpu.roll(tile, (2 * q + 1) % 128, 1), packed)
        packed = jnp.where(lane == 2 * q + 1, pltpu.roll(tile, (2 * q + 3) % 128, 1), packed)
    first = 2 * ntr * nlev
    for k in range(nlev):
        packed = jnp.where(lane == first + k, pltpu.roll(v_ref[k, :, top:], first + k + 1, 1), packed)
    ocean = land_ref[...].astype(jnp.float32)
    packed = jnp.where(lane == first + nlev, pltpu.roll(ocean[:, top:], first + nlev + 1, 1), packed)
    fold_out[...] = packed
    pl.semaphore_wait(barrier, len(partners))

    copies = []

    def send_to(src, dst, other):
        n = len(copies)
        copies.append(pltpu.make_async_remote_copy(
            src_ref=src, dst_ref=dst, send_sem=send.at[n], recv_sem=recv.at[n], device_id=other, device_id_type=MESH,
        ))
        copies[-1].start()
        return copies[-1]

    last = cols - 8
    sent_fold = [send_to(fold_out, fold_in, fold)]
    sent_lev = [send_to(up_out, up_in, below), send_to(down_out, down_in, above), send_to(w_ref.at[nlev - 1], w_in, below)]
    sent_side = [
        send_to(tr.at[:, :, pl.ds(last, 8)], west_tr, east),
        send_to(tr.at[:, :, pl.ds(0, 8)], east_tr, west),
        send_to(u_ref.at[:, pl.ds(last, 8)], west_u, east),
        send_to(land_ref.at[pl.ds(last, 8)], west_land, east),
        send_to(land_ref.at[pl.ds(0, 8)], east_land, west),
    ]
    sent_table = [
        send_to(tab_ref.at[h * 8 + row], tab_in.at[h * 8 + NEAR[o]], other) for o, h, row, other in table_to
    ]

    for copy in sent_fold:
        copy.wait_recv()
    for i in range(cols):
        mirrored[cols - 1 - i : cols - i, :] = fold_in[i : i + 1, :]
    ghosts = mirrored[...]
    wide = rows + 128
    wide_lane = lax.broadcasted_iota(jnp.int32, (cols, rows), 1)
    nothing = jnp.zeros((cols, 128), jnp.float32)

    def ahead(a, axis):
        return pltpu.roll(a, a.shape[axis] - 1, axis)

    def behind(a, axis):
        return pltpu.roll(a, 1, axis)

    ocean_wide = jnp.concatenate(
        [ocean, jnp.where(lane == 0, pltpu.roll(ghosts, 128 - first - nlev, 1), 0.0)], 1
    )
    open_north = ocean_wide * ahead(ocean_wide, 1)
    for k in range(nlev):
        v = v_ref[k]
        other = pltpu.roll(ghosts, (127 - first - k) % 128, 1)
        fixed = jnp.where(lane == 127, 0.5 * (v[:, top:] - other), v[:, top:])
        courant = jnp.concatenate([v[:, :top], fixed, nothing], 1)
        coefs = coefficients(courant, open_north)
        for t in range(ntr):
            q = t * nlev + k
            ghost = pltpu.roll(ghosts, (128 - 2 * q) % 128, 1)
            x = jnp.concatenate([tr[t, k], jnp.where(lane < 2, ghost, 0.0)], 1)
            beyond = ahead(x, 1)
            step = beyond - x
            slope = minmod(behind(step, 1), step)
            north = flux(coefs, x, slope, beyond, ahead(slope, 1))
            div[t, k] = (north - behind(north, 1))[:, :rows]

    for copy in sent_side:
        copy.wait_recv()
    ocean_tall = jnp.concatenate(
        [west_land[...].astype(jnp.float32), ocean, east_land[...].astype(jnp.float32)], 0
    )
    open_east = ocean_tall * ahead(ocean_tall, 0)
    for k in range(nlev):
        u = u_ref[k]
        courant = jnp.concatenate([west_u[k], u, jnp.zeros((8, rows), jnp.float32)], 0)
        coefs = coefficients(courant, open_east)
        for t in range(ntr):
            x = jnp.concatenate([west_tr[t, k], tr[t, k], east_tr[t, k]], 0)
            beyond = ahead(x, 0)
            step = beyond - x
            slope = minmod(behind(step, 0), step)
            out = flux(coefs, x, slope, beyond, ahead(slope, 0))
            div[t, k] += (out - behind(out, 0))[8 : 8 + cols]

    for copy in sent_lev:
        copy.wait_recv()
    not_first = jnp.where(lev > 0, 1.0, 0.0).astype(jnp.float32)
    not_last = jnp.where(lev < levs - 1, 1.0, 0.0).astype(jnp.float32)
    for i0 in range(0, cols, 8):
        part = slice(i0, i0 + 8)
        open_part = land_ref[part, :].astype(jnp.float32)
        coefs = [coefficients(w_in[part, :], open_part * not_first)]
        for k in range(nlev):
            coefs.append(coefficients(w_ref[k, part, :], open_part * not_last if k == nlev - 1 else open_part))
        for t in range(ntr):
            cells = [up_in[t, m, part, :].astype(jnp.float32) * not_first for m in range(2)]
            cells += [tr[t, k, part, :] for k in range(nlev)]
            cells += [down_in[t, m, part, :].astype(jnp.float32) * not_last for m in range(2)]
            steps = [b - a for a, b in zip(cells[:-1], cells[1:])]
            slopes = [minmod(a, b) for a, b in zip(steps[:-1], steps[1:])]
            faces = [
                flux(coefs[f], cells[f + 1], slopes[f], cells[f + 2], slopes[f + 1]) for f in range(nlev + 1)
            ]
            for k in range(nlev):
                total = div[t, k, part, :] + (faces[k + 1] - faces[k])
                new = cells[k + 2] - total
                new_ref[t, k, part, :] = new
                q = t * nlev + k
                for kind, value in ((0, new), (1, total)):
                    for m in range(rows // 128):
                        at = (i0 * (rows // 128) + m) * GROUP + q
                        staged[kind, pl.ds(at, 8, stride=GROUP * (rows // 128)), :] = value[:, m * 128 : m * 128 + 128]

    for kind in range(2):
        for b in range(BLOCKS):
            for m in range(SB // 128):
                at = (b * (SB // 128) + m) * GROUP
                x_ref[kind, b, :, m * 128 : m * 128 + 128] = staged[kind, at : at + GROUP, :].astype(jnp.bfloat16)

    for copy in sent_table:
        copy.wait_recv()
    for h, row in ((0, z), (1, y)):
        tab_out[h * 8 : h * 8 + 1, :] = tab_ref[h * 8 + row, 0:1, :]
        for j in range(1, 8):
            tab_out[h * 8 + j : h * 8 + j + 1, :] = tab_in[h * 8 + j, 0:1, :]
    for copy in copies:
        copy.wait_send()


def advect(tracers, u, v, w, land, table):
    vmem = pl.BlockSpec(memory_space=pltpu.VMEM)
    f32, bf16 = jnp.float32, jnp.bfloat16
    ntr, nlev, cols, rows = tracers.shape
    messages = 1 + 3 + 5 + 14
    return pl.pallas_call(
        advect_kernel,
        out_shape=[
            jax.ShapeDtypeStruct(tracers.shape, f32),
            jax.ShapeDtypeStruct((2, BLOCKS, GROUP, SB), bf16),
            jax.ShapeDtypeStruct((16, 128), jnp.int32),
        ],
        in_specs=[vmem] * 6,
        out_specs=[vmem] * 3,
        scratch_shapes=[
            pltpu.VMEM((ntr, 2, cols, rows), bf16),
            pltpu.VMEM((ntr, 2, cols, rows), bf16),
            pltpu.VMEM((ntr, 2, cols, rows), bf16),
            pltpu.VMEM((ntr, 2, cols, rows), bf16),
            pltpu.VMEM((cols, rows), f32),
            pltpu.VMEM((ntr, nlev, 8, rows), f32),
            pltpu.VMEM((ntr, nlev, 8, rows), f32),
            pltpu.VMEM((nlev, 8, rows), f32),
            pltpu.VMEM((8, rows), jnp.int32),
            pltpu.VMEM((8, rows), jnp.int32),
            pltpu.VMEM((cols, 128), f32),
            pltpu.VMEM((cols, 128), f32),
            pltpu.VMEM((cols, 128), f32),
            pltpu.VMEM((16, 8, 128), jnp.int32),
            pltpu.VMEM((ntr, nlev, cols, rows), f32),
            pltpu.VMEM((2, BLOCKS * SB // 128 * GROUP, 128), f32),
            pltpu.SemaphoreType.DMA((messages,)),
            pltpu.SemaphoreType.DMA((messages,)),
        ],
        compiler_params=pltpu.CompilerParams(
            collective_id=2, has_side_effects=True, vmem_limit_bytes=32 * 1024 * 1024
        ),
        cost_estimate=pl.CostEstimate(flops=12_000_000, bytes_accessed=4_000_000, transcendentals=0),
    )(tracers, u, v, w, land, table)


def slot_tables(src_block, dst_tile, dst_block, pattern):
    me = lax.axis_index("tile")
    y, z, c = me // 16, (me // 2) % 8, me % 2
    targets = dst_tile[:, 0]
    order = jnp.arange(targets.shape[0], dtype=jnp.int32)
    same = (targets[:, None] == targets[None, :]) & (order[None, :] < order[:, None])
    rank = jnp.sum(same.astype(jnp.int32), 1)
    ty, tz, tc = targets // 16, (targets // 2) % 8, targets % 2
    low = (tc ^ c) * 2 + rank
    by_z = tz * SLOTS + ((ty - y) % 8) * 4 + low
    by_y = ty * SLOTS + ((tz - z) % 8) * 4 + low
    slot = jnp.stack([by_z, by_y])
    hit = slot[:, None, :] == jnp.arange(8 * SLOTS, dtype=jnp.int32)[None, :, None]
    values = jnp.stack([src_block, pattern, dst_block, jnp.zeros_like(pattern)]) + 1
    table = jnp.sum(jnp.where(hit[:, None], values[None, :, None, :], 0), 3) - 1
    table = table.reshape(2, 4, 8, SLOTS).transpose(0, 2, 1, 3).reshape(16, 1, 128)
    return jnp.broadcast_to(table, (16, 8, 128))


def shards(
    tracers,
    u_courant,
    v_courant,
    w_courant,
    land_mask,
    weights,
    src_block,
    dst_tile,
    dst_block,
    pattern,
):
    table = slot_tables(src_block, dst_tile, dst_block, pattern)
    new_tracers, payload, tables = advect(tracers, u_courant, v_courant, w_courant, land_mask, table)
    fields, fluxes = remap(payload, weights, tables)
    shape = tracers.shape[:2] + (NBD * DB,)
    return (new_tracers, fields.reshape(shape), fluxes.reshape(shape))


def solution(mesh):
    in_specs = (
        P(None, "lev", "tile", None),
        P("lev", "tile", None),
        P("lev", "tile", None),
        P("lev", "tile", None),
        P("tile", None),
        P(),
        P("tile"),
        P("tile", None),
        P("tile"),
        P("tile"),
    )
    out_specs = (P(None, "lev", "tile", None), P(None, "lev", "tile"), P(None, "lev", "tile"))
    return jax.shard_map(shards, mesh=mesh, in_specs=in_specs, out_specs=out_specs, check_vma=False)
```

time: 193 us -> 106 us (0.55)
  blocking collectives: 48.2 us -> 0 us
  local copies, waits for them, and re-layouts: 39.5 us -> 7.32 us
  Pallas kernels: 66.4 us -> 95.1 us
  starting transfers between devices: 25.4 us -> 0 us
  other arithmetic: 10.8 us -> 2.71 us
    all_gather x1 -> x0, blocking collectives: 48.2 us -> none  [shards(): lax.all_gather(slot_tables(src_block, dst_tile, dst_block, pattern), 'tile')]
    reshape x3 -> x0, local copies, waits for them, and re-layouts: 26.9 us -> none  [the longest x1 26.7 us: local_tables(): full = gathered.reshape(8, 8, 2, 3, 8, 8, 2, 2)]
    pallas_call x0 -> x1, Pallas kernels: none -> 25.5 us  [advect(): pl.pallas_call(advect_kernel, out_shape=[jax.ShapeDtypeStruct(tracers.sha...]
    ppermute x5 -> x0, starting transfers between devices: 25.4 us -> none  [the longest x1 11.9 us: shards(): lax.ppermute(top_rows, 'tile', [(i, strips - 1 - i) for i in range(strips)])]
    dynamic_slice x4 -> x0, local copies, waits for them, and re-layouts: 5.47 us -> none  [the longest x2 3.6 us: local_tables(): by_y = lax.dynamic_index_in_dim(by_y, y, 2, keepdims=False)]
    unnamed x22 -> x11, local copies, waits for them, and re-layouts: 1.42 us -> 5.58 us
    mul x10 -> x0, other arithmetic: 3.95 us -> none  [the longest x4 3.72 us: face_flux(): return opening * (upwind + downwind)]
    pallas_call x1, Pallas kernels: 66.4 us -> 69.6 us  [remap(): pl.pallas_call(remap_kernel, out_shape=[jax.ShapeDtypeStruct((GROUP, NBD...]
  transfers between devices with their start and end apart: 5 -> 0, of which waited for: 0 -> 0; matrix products, arithmetic and copies ran while one was open for 21% -> 0% of each run, Pallas kernels for 0% -> 0%
where the time goes in v2:
time: 106 us
  Pallas kernels  95.1 us (90%)
  local copies, waits for them, and re-layouts  7.32 us (7%)
  other arithmetic  2.71 us (3%)
    pallas_call x1, Pallas kernels, remap(): pl.pallas_call(remap_kernel, out_shape=[jax.ShapeDtypeStruct((GROUP, NBD...  69.6 us
    pallas_call x1, Pallas kernels, advect(): pl.pallas_call(advect_kernel, out_shape=[jax.ShapeDtypeStruct(tracers.sha...  25.5 us
    unnamed x11, local copies, waits for them, and re-layouts  5.58 us

profile of v2, /device:TPU:1, one launch (start us, length us, event | category | flops | bytes accessed | tf_op | source)
XLA Modules:
  0.0 105.9 jit_solution(17445200655399953776)
XLA Ops:
  0.7 0.9 convert_reduce_fusion
  1.6 0.7 fusion.3
  2.4 0.7 add_add_fusion
  3.1 0.4 select_reduce_fusion
  3.4 0.1 sub.58
  3.5 0.1 broadcast_in_dim.36
  3.6 0.0 copy-start
  3.6 1.1 %copy-done = f32[4,4,32,384]{3,2,1,0:T(8,128)S(1)} copy-done((f32[4,4,32,384]{3,2,1,0:T(8,128)S(1)}, f32[4,4,32,384]{3,2,1,0:T(8,128)}, u32[]{:S(2)}) %copy-start) | copy-done | bytes 786456
  4.7 0.0 copy-start.1
  4.8 0.9 copy-done.1
  5.7 0.0 copy-start.2
  5.7 0.9 copy-done.2
  6.6 0.0 copy-start.3
  6.6 0.9 copy-done.3
  7.5 0.0 copy-start.4
  7.5 0.8 copy-done.4
  8.3 25.5 %shard_map.121 = (f32[4,4,32,384]{3,2,1,0:T(8,128)S(1)}, bf16[2,24,16,512]{3,2,1,0:T(8,128)(2,1)S(1)}, s32[16,128]{1,0:T(8,128)S(1)}) custom-call(f32[4,4,32,384]{3,2,1,0:T(8,128)S(1)} %copy-done, f32[4,32,384]{2,1,0:T(8,128)S(1)} %copy-done.1, f32[4,32,384]{2,1,0:T(8,128)S(1)} %copy-done.2, f32[4,32,384]{2,1,0:T(8,128)S(1)} %copy-done.3, ...), custom_call_target="tpu_custom_call" | custom-call | flops 12000000 | bytes 4000000 | tf_op jit(solution)/shard_map/pallas_call | solution.py:411
  33.8 69.6 %shard_map.122 = (f32[16,4096]{1,0:T(8,128)S(1)}, f32[16,4096]{1,0:T(8,128)S(1)}) custom-call(bf16[2,24,16,512]{3,2,1,0:T(8,128)(2,1)S(1)} %get-tuple-element.9.x_ref, bf16[8,512,256]{2,1,0:T(8,128)(2,1)} %w_ref.3, s32[16,128]{1,0:T(8,128)S(1)} %get-tuple-element.10.tab_ref), custom_call_target="tpu_custom_call" | custom-call | flops 12999999488 | bytes 4000000 | tf_op jit(solution)/shard_map/pallas_call | solution.py:200
  103.5 0.8 reshape.339
  104.2 0.8 reshape.340
  105.0 0.9 copy.16
  (7 shorter events, 0.1 us)
Async XLA Ops:
  3.6 1.1 %copy-start = (f32[4,4,32,384]{3,2,1,0:T(8,128)S(1)}, f32[4,4,32,384]{3,2,1,0:T(8,128)}, u32[]{:S(2)}) copy-start(f32[4,4,32,384]{3,2,1,0:T(8,128)} %tr.1) | copy-start | bytes 2359300
  4.7 0.9 copy-start.1
  5.7 0.9 copy-start.2
  6.6 0.9 copy-start.3
  7.5 0.8 copy-start.4

commit v3 on v0

v3 whole, which is shorter than its diff:
```python
import jax
import jax.numpy as jnp
from jax import lax
from jax.experimental import pallas as pl
from jax.experimental.pallas import tpu as pltpu
from jax.sharding import PartitionSpec as P

MESH = pl.DeviceIdType.MESH
RING = 8
NBD = 16
GROUP = 16
BLOCKS = 24
SB = 512
DB = 256
PATTERNS = 8
SLOTS = 32
PARTS = 4
HALVES = (range(0, PARTS // 2), range(PARTS // 2, PARTS))


def minmod(first, second):
    return jnp.maximum(jnp.minimum(first, second), jnp.minimum(jnp.maximum(first, second), 0.0))


def coefficients(courant, opening):
    up, down = jnp.maximum(courant, 0.0) * opening, jnp.minimum(courant, 0.0) * opening
    return up, up * (0.5 * (1.0 - courant)), down, down * (0.5 * (1.0 + courant))


def flux(coefs, left, left_slope, right, right_slope):
    up, up_slope, down, down_slope = coefs
    return (up * left + up_slope * left_slope) + (down * right - down_slope * right_slope)


NEAR = {1: 1, 2: 3, 3: 5, 4: 7, 5: 6, 6: 4, 7: 2}


def slot_tables(tab_src, y, z, c, src_ref, tile_ref, block_ref, pattern_ref):
    entries = tile_ref.shape[1]
    targets = tile_ref[...]
    square = (entries, entries)
    row_i = lax.broadcasted_iota(jnp.int32, square, 0)
    lane_i = lax.broadcasted_iota(jnp.int32, square, 1)
    as_rows = jnp.broadcast_to(targets.astype(jnp.float32), square)
    same = jnp.where((jnp.transpose(as_rows) == as_rows) & (row_i < lane_i), 1.0, 0.0)
    rank = jnp.sum(same, axis=0, keepdims=True).astype(jnp.int32)
    ty, tz, tc = targets >> 4, (targets >> 1) & 7, targets & 1
    low = jnp.bitwise_xor(tc, c) * 2 + rank
    value, slot_i = row_i // SLOTS, lax.rem(row_i, SLOTS)
    named = jnp.where(value == 0, src_ref[...] + 1, jnp.where(value == 1, pattern_ref[...] + 1, block_ref[...] + 1))
    named = jnp.where(value == 3, 0, named).astype(jnp.float32)
    place_i = lax.broadcasted_iota(jnp.int32, (16, entries), 0)
    for h, place, slot in ((0, tz, ((ty - y) & 7) * 4 + low), (1, ty, ((tz - z) & 7) * 4 + low)):
        filled = jnp.where(slot == slot_i, named, 0.0).astype(jnp.bfloat16)
        chosen = jnp.where(place == place_i, 1.0, 0.0).astype(jnp.bfloat16)
        table = lax.dot_general(chosen, filled, (((1,), (1,)), ((), ())), preferred_element_type=jnp.float32)
        table = table.astype(jnp.int32) - 1
        for p in range(8):
            tab_src[h * 8 + p] = jnp.broadcast_to(table[p : p + 1, :], (8, 128))


def kernel(
    tr_hbm, u_hbm, v_hbm, w_hbm, land_hbm, weights_hbm, src_ref, tile_ref, block_ref, pattern_ref,
    new_ref, out0, out1,
    tr, u_ref, v_ref, w_ref, land_ref, weights,
    up_out, down_out, up_in, down_in, w_in, west_tr, east_tr, west_u, west_land, east_land,
    fold_out, fold_in, mirrored, tab_src, tab_in, tab, tab_s, div, staged,
    x_ref, ag, prod, terms, terms_out, masks, acc, rs_out, rs_in,
    load, send, recv, ag_send, ag_recv, sib_send, sib_recv, rs_send, rs_recv,
):
    tiles, levs = lax.axis_size("tile"), lax.axis_size("lev")
    me, lev = lax.axis_index("tile"), lax.axis_index("lev")
    y, z, c = me // 16, lax.rem(me // 2, 8), lax.rem(me, 2)
    ntr, nlev, cols, rows = tr.shape

    def strip(yy, zz, cc):
        return {"tile": yy * 16 + zz * 2 + cc}

    east, west = {"tile": lax.rem(me + 1, tiles)}, {"tile": lax.rem(me + tiles - 1, tiles)}
    fold = {"tile": tiles - 1 - me}
    below, above = {"lev": lax.rem(lev + 1, levs)}, {"lev": lax.rem(lev + levs - 1, levs)}
    sibling = strip(y, z, 1 - c)
    table_to = []
    for o in range(1, 8):
        zz, yy = lax.rem(z + o, 8), lax.rem(y + o, 8)
        table_to.append((o, 0, zz, strip(y, zz, c)))
        table_to.append((o, 1, yy, strip(yy, z, c)))
    partners = [east, west, fold, below, above] + [entry[3] for entry in table_to]
    along_z = (strip(y, lax.rem(z + 1, RING), c), strip(y, lax.rem(z + RING - 1, RING), c))
    along_y = (strip(lax.rem(y + 1, RING), z, c), strip(lax.rem(y + RING - 1, RING), z, c))
    gather_to = (along_z, along_y)
    reduce_to = (along_y, along_z)

    barrier = pltpu.get_barrier_semaphore()
    for other in partners:
        pl.semaphore_signal(barrier, inc=1, device_id=other, device_id_type=MESH)
    loads = [
        pltpu.make_async_copy(src, dst, load.at[n])
        for n, (src, dst) in enumerate((
            (tr_hbm, tr), (land_hbm, land_ref), (v_hbm, v_ref), (u_hbm, u_ref), (w_hbm, w_ref), (weights_hbm, weights)
        ))
    ]
    for copy in loads[:5]:
        copy.start()
    slot_tables(tab_src, y, z, c, src_ref, tile_ref, block_ref, pattern_ref)
    loads[0].wait()
    down_out[...] = tr[:, 0:2].astype(jnp.bfloat16)
    up_out[...] = tr[:, nlev - 2 : nlev].astype(jnp.bfloat16)
    for n in range(1, 5):
        loads[n].wait()
    lane = lax.broadcasted_iota(jnp.int32, (cols, 128), 1)
    top = rows - 128
    packed = jnp.zeros((cols, 128), jnp.float32)
    for q in range(ntr * nlev):
        tile = tr[q // nlev, q % nlev, :, top:]
        packed = jnp.where(lane == 2 * q, pltpu.roll(tile, (2 * q + 1) % 128, 1), packed)
        packed = jnp.where(lane == 2 * q + 1, pltpu.roll(tile, (2 * q + 3) % 128, 1), packed)
    first = 2 * ntr * nlev
    for k in range(nlev):
        packed = jnp.where(lane == first + k, pltpu.roll(v_ref[k, :, top:], first + k + 1, 1), packed)
    ocean = land_ref[...].astype(jnp.float32)
    packed = jnp.where(lane == first + nlev, pltpu.roll(ocean[:, top:], first + nlev + 1, 1), packed)
    fold_out[...] = packed
    pl.semaphore_wait(barrier, len(partners))

    copies = []
    started = []

    def start(copy):
        copy.start()
        started.append(copy)

    def send_to(src, dst, other):
        n = len(copies)
        copies.append(pltpu.make_async_remote_copy(
            src_ref=src, dst_ref=dst, send_sem=send.at[n], recv_sem=recv.at[n], device_id=other, device_id_type=MESH,
        ))
        start(copies[-1])
        return copies[-1]

    last, middle = cols - 8, cols // 2
    sent_fold = [send_to(fold_out, fold_in, fold)]
    sent_side = [
        send_to(tr.at[:, :, pl.ds(last, 8)], west_tr, east),
        send_to(tr.at[:, :, pl.ds(0, 8)], east_tr, west),
        send_to(u_ref.at[:, pl.ds(last, 8)], west_u, east),
        send_to(land_ref.at[pl.ds(last, 8)], west_land, east),
        send_to(land_ref.at[pl.ds(0, 8)], east_land, west),
    ]
    sent_lev = []
    for at in (pl.ds(0, middle), pl.ds(middle, middle)):
        sent_lev.append([
            send_to(up_out.at[:, :, at], up_in.at[:, :, at], below),
            send_to(down_out.at[:, :, at], down_in.at[:, :, at], above),
            send_to(w_ref.at[nlev - 1, at], w_in.at[at], below),
        ])
    sent_table = [
        send_to(tab_src.at[h * 8 + row], tab_in.at[h * 8 + NEAR[o]], other) for o, h, row, other in table_to
    ]

    loads[5].start()

    def ahead(a, axis):
        return pltpu.roll(a, a.shape[axis] - 1, axis)

    def behind(a, axis):
        return pltpu.roll(a, 1, axis)

    for copy in sent_side:
        copy.wait_recv()
    ocean_tall = jnp.concatenate(
        [west_land[...].astype(jnp.float32), ocean, east_land[...].astype(jnp.float32)], 0
    )
    open_east = ocean_tall * ahead(ocean_tall, 0)
    for k in range(nlev):
        courant = jnp.concatenate([west_u[k], u_ref[k], jnp.zeros((8, rows), jnp.float32)], 0)
        coefs = coefficients(courant, open_east)
        for t in range(ntr):
            x = jnp.concatenate([west_tr[t, k], tr[t, k], east_tr[t, k]], 0)
            beyond = ahead(x, 0)
            step = beyond - x
            slope = minmod(behind(step, 0), step)
            out = flux(coefs, x, slope, beyond, ahead(slope, 0))
            div[t, k] = (out - behind(out, 0))[8 : 8 + cols]

    for copy in sent_table:
        copy.wait_recv()
    for h, row in ((0, z), (1, y)):
        tab[h * 8 : h * 8 + 1, :] = tab_src[h * 8 + row, 0:1, :]
        for j in range(1, 8):
            tab[h * 8 + j : h * 8 + j + 1, :] = tab_in[h * 8 + j, 0:1, :]
    sent_tables = send_to(tab.at[pl.ds(0, 16)], tab.at[pl.ds(16, 16)], sibling)

    for copy in sent_fold:
        copy.wait_recv()
    for i in range(cols):
        mirrored[cols - 1 - i : cols - i, :] = fold_in[i : i + 1, :]
    ghosts = mirrored[...]
    nothing = jnp.zeros((cols, 128), jnp.float32)
    ocean_wide = jnp.concatenate(
        [ocean, jnp.where(lane == 0, pltpu.roll(ghosts, 128 - first - nlev, 1), 0.0)], 1
    )
    open_north = ocean_wide * ahead(ocean_wide, 1)

    def north_part(part):
        for k in range(nlev):
            v = v_ref[k, part, :]
            other = pltpu.roll(ghosts[part], (127 - first - k) % 128, 1)
            fixed = jnp.where(lane[part] == 127, 0.5 * (v[:, top:] - other), v[:, top:])
            courant = jnp.concatenate([v[:, :top], fixed, nothing[part]], 1)
            coefs = coefficients(courant, open_north[part])
            for t in range(ntr):
                ghost = pltpu.roll(ghosts[part], (128 - 2 * (t * nlev + k)) % 128, 1)
                x = jnp.concatenate([tr[t, k, part, :], jnp.where(lane[part] < 2, ghost, 0.0)], 1)
                beyond = ahead(x, 1)
                step = beyond - x
                slope = minmod(behind(step, 1), step)
                north = flux(coefs, x, slope, beyond, ahead(slope, 1))
                div[t, k, part, :] += (north - behind(north, 1))[:, :rows]

    streams = [(h, d) for h in range(2) for d in range(2)]
    quarter = BLOCKS // 4

    def gather_copy(h, d, n):
        k, sub = (n // 4 + 1, n % 4) if n < 12 else (4, 2 * d + n - 12)
        blocks = pl.ds(quarter * sub, quarter)
        src = x_ref.at[h, blocks] if k == 1 else ag.at[h, d, k - 2, blocks]
        dst = ag.at[h, 0 if k == 4 else d, k - 1, blocks]
        return pltpu.make_async_remote_copy(
            src_ref=src, dst_ref=dst, send_sem=ag_send.at[h, d, n], recv_sem=ag_recv.at[h, d, n],
            device_id=gather_to[h][d], device_id_type=MESH,
        )

    not_first = jnp.where(lev > 0, 1.0, 0.0).astype(jnp.float32)
    not_last = jnp.where(lev < levs - 1, 1.0, 0.0).astype(jnp.float32)
    across = rows // 128
    for i0 in range(0, cols, 8):
        part = slice(i0, i0 + 8)
        north_part(part)
        if i0 % middle == 0:
            for copy in sent_lev[i0 // middle]:
                copy.wait_recv()
        open_part = land_ref[part, :].astype(jnp.float32)
        coefs = [coefficients(w_in[part, :], open_part * not_first)]
        for k in range(nlev):
            coefs.append(coefficients(w_ref[k, part, :], open_part * not_last if k == nlev - 1 else open_part))
        for t in range(ntr):
            cells = [up_in[t, m, part, :].astype(jnp.float32) * not_first for m in range(2)]
            cells += [tr[t, k, part, :] for k in range(nlev)]
            cells += [down_in[t, m, part, :].astype(jnp.float32) * not_last for m in range(2)]
            steps = [b - a for a, b in zip(cells[:-1], cells[1:])]
            slopes = [minmod(a, b) for a, b in zip(steps[:-1], steps[1:])]
            faces = [
                flux(coefs[f], cells[f + 1], slopes[f], cells[f + 2], slopes[f + 1]) for f in range(nlev + 1)
            ]
            for k in range(nlev):
                total = div[t, k, part, :] + (faces[k + 1] - faces[k])
                new = cells[k + 2] - total
                new_ref[t, k, part, :] = new
                q = t * nlev + k
                for kind, value in ((0, new), (1, total)):
                    for m in range(across):
                        at = (i0 * across + m) * GROUP + q
                        staged[kind, pl.ds(at, 8, stride=GROUP * across), :] = value[:, m * 128 : m * 128 + 128]
        for kind in range(2):
            for b in range(i0 * rows // SB, (i0 + 8) * rows // SB):
                for m in range(SB // 128):
                    at = (b * (SB // 128) + m) * GROUP
                    x_ref[kind, b, :, m * 128 : m * 128 + 128] = staged[kind, at : at + GROUP, :].astype(jnp.bfloat16)
        for h, d in streams:
            start(gather_copy(h, d, i0 // 8))

    sent_tables.wait_recv()
    to_scalars = pltpu.make_async_copy(tab, tab_s, load.at[6])
    to_scalars.start()
    to_scalars.wait()
    lanes = 2 * 8 * 2 * GROUP
    sub_i = lax.broadcasted_iota(jnp.int32, (NBD * GROUP, lanes), 0)
    lane_i = lax.broadcasted_iota(jnp.int32, (NBD * GROUP, lanes), 1)
    wanted = jnp.where(lax.rem(sub_i, GROUP) == lax.rem(lane_i, GROUP), sub_i // GROUP, -2)
    slot_of_lane = lax.broadcasted_iota(jnp.int32, (1, lanes), 1) // GROUP

    def one_mask(i, carry):
        h, q = i // 8, lax.rem(i, 8)
        blocks = jnp.full((1, lanes), -1, jnp.int32)
        for core in range(2):
            for j in range(8):
                for r in range(2):
                    named = tab_s[core * 16 + h * 8 + j, 2 * SLOTS + q * 4 + core * 2 + r]
                    blocks = jnp.where(slot_of_lane == (core * 8 + j) * 2 + r, named, blocks)
        masks[i] = jnp.where(blocks == wanted, 1.0, 0.0).astype(jnp.bfloat16)
        return carry

    lax.fori_loop(0, 16, one_mask, 0)
    loads[5].wait()

    def sibling_copy(h, j):
        at = pl.ds((8 + j) * 2 * GROUP, 2 * GROUP)
        return pltpu.make_async_remote_copy(
            src_ref=terms_out.at[h, j], dst_ref=terms.at[pl.ds(h * 8, 8), at],
            send_sem=sib_send.at[h, j], recv_sem=sib_recv.at[h, j], device_id=sibling, device_id_type=MESH,
        )

    def multiply(view, b0, count):
        x = view[b0 : b0 + count].reshape(count * GROUP, SB)

        def one_pattern(p, carry):
            r = jnp.dot(x, weights[p], preferred_element_type=jnp.float32)
            prod[pl.ds(p * BLOCKS + b0, count)] = r.astype(jnp.bfloat16).reshape(count, GROUP, DB)
            return carry

        lax.fori_loop(0, PATTERNS, one_pattern, 0, unroll=PATTERNS)

    def pick(h, j):
        def product(slot):
            src, pat = tab_s[h * 8 + j, slot], tab_s[h * 8 + j, SLOTS + slot]
            return prod[jnp.clip(pat * BLOCKS + src, 0, PATTERNS * BLOCKS - 1)]

        def one_target(q, carry):
            for r in range(2):
                terms_out[h, j, q, r * GROUP : (r + 1) * GROUP, :] = product(q * 4 + 2 + r)
            for r in range(2):
                at = (j * 2 + r) * GROUP
                terms[h * 8 + q, at : at + GROUP, :] = product(q * 4 + r)
            return carry

        lax.fori_loop(0, 8, one_target, 0, unroll=4)
        start(sibling_copy(h, j))

    def arrived(h, j):
        k, d = (j + 1) // 2, (j + 1) % 2
        multiply(x_ref.at[h] if j == 0 else ag.at[h, d, k - 1], 0, BLOCKS)
        pick(h, j)

    waiting = [(0, 0), (1, 0)]
    for n in range(12):
        for h, d in streams:
            gather_copy(h, d, n).wait_recv()
            if n < 8:
                start(gather_copy(h, d, n + 4))
            elif (n - 8) // 2 == d:
                start(gather_copy(h, d, 12 + (n - 8) % 2))
        if waiting:
            arrived(*waiting.pop(0))
        if n % 4 == 3:
            k = n // 4 + 1
            waiting += [(0, 2 * k - 1), (0, 2 * k), (1, 2 * k - 1), (1, 2 * k)]
    while waiting:
        arrived(*waiting.pop(0))
    for h in range(2):
        for n in (12, 13):
            for d in range(2):
                gather_copy(h, d, n).wait_recv()
        multiply(ag.at[h, 0, 3], 0, BLOCKS)
        pick(h, 7)

    size = NBD * GROUP // PARTS

    def partial(h, *targets):
        for q in targets:
            acc[h, q] = jnp.dot(masks[h * 8 + q], terms[h * 8 + q], preferred_element_type=jnp.float32)

    def reduce_copy(h, d, s, part):
        at = pl.ds(part * size, size)
        n = PARTS * s + part
        return pltpu.make_async_remote_copy(
            src_ref=rs_out.at[h, d, s, at], dst_ref=rs_in.at[h, d, s, at],
            send_sem=rs_send.at[h, d, n], recv_sem=rs_recv.at[h, d, n],
            device_id=reduce_to[h][d], device_id_type=MESH,
        )

    def came(h, d, s, part, at):
        reduce_copy(h, d, s, part).wait_recv()
        return rs_in[h, d, s, at].astype(jnp.float32)

    def pass_on(h, d, s, part):
        at = pl.ds(part * size, size)
        total = acc[h, 4 - s if d == 0 else 4 + s, at]
        if s > 1 or (s == 1 and part in HALVES[d]):
            total += came(h, d, s - 1, part, at)
        rs_out[h, d, s, at] = total.astype(jnp.bfloat16)
        start(reduce_copy(h, d, s, part))

    order = [[*HALVES[1 - d], *HALVES[d]] for d in range(2)]
    for h in range(2):
        for j in range(8):
            sibling_copy(h, j).wait_recv()
        partial(h, 4)
        for p in range(PARTS // 2):
            for d in range(2):
                pass_on(h, d, 0, HALVES[d][p])
    for h in range(2):
        partial(h, 3, 5)
        for p in range(PARTS // 2):
            for d in range(2):
                pass_on(h, d, 1, order[d][p])
    for h in range(2):
        partial(h, 2, 6)
    for p in range(PARTS // 2, PARTS):
        for h, d in streams:
            pass_on(h, d, 1, order[d][p])
    for h in range(2):
        partial(h, 1, 7)
    for p in range(PARTS):
        for h, d in streams:
            pass_on(h, d, 2, order[d][p])
    for h in range(2):
        partial(h, 0)
    for p in range(PARTS):
        for h, d in streams:
            pass_on(h, d, 3, order[d][p])
    for p in range(PARTS):
        for h, out in ((0, out0), (1, out1)):
            part = order[0][p]
            at = pl.ds(part * size, size)
            total = acc[h, 0, at] + came(h, 0, 3, part, at) + came(h, 1, 3, part, at)
            for i in range(size // GROUP):
                b = part * (size // GROUP) + i
                for t in range(ntr):
                    at_row = i * GROUP + t * nlev
                    out[t, :, b * DB : (b + 1) * DB] = total[at_row : at_row + nlev]
    for copy in started:
        copy.wait_send()


def deliver(new_in, fields_in, fluxes_in, new_out, fields_out, fluxes_out, done):
    pairs = ((new_in, new_out), (fields_in, fields_out), (fluxes_in, fluxes_out))
    copies = [pltpu.make_async_copy(src, dst, done.at[n]) for n, (src, dst) in enumerate(pairs)]
    for copy in copies:
        copy.start()
    for copy in copies:
        copy.wait()


def shards(
    tracers,
    u_courant,
    v_courant,
    w_courant,
    land_mask,
    weights,
    src_block,
    dst_tile,
    dst_block,
    pattern,
):
    vmem = pl.BlockSpec(memory_space=pltpu.VMEM)
    anywhere = pl.BlockSpec(memory_space=pl.ANY)
    f32, bf16, i32 = jnp.float32, jnp.bfloat16, jnp.int32
    ntr, nlev, cols, rows = tracers.shape
    height = NBD * GROUP
    dma = pltpu.SemaphoreType.DMA
    messages = 1 + 5 + 6 + 14 + 1
    new_tracers, fields, fluxes = pl.pallas_call(
        kernel,
        out_shape=[
            jax.ShapeDtypeStruct(tracers.shape, f32),
            jax.ShapeDtypeStruct((ntr, nlev, NBD * DB), f32),
            jax.ShapeDtypeStruct((ntr, nlev, NBD * DB), f32),
        ],
        in_specs=[anywhere] * 6 + [vmem] * 4,
        out_specs=[vmem] * 3,
        scratch_shapes=[
            pltpu.VMEM(tracers.shape, f32),
            pltpu.VMEM((nlev, cols, rows), f32),
            pltpu.VMEM((nlev, cols, rows), f32),
            pltpu.VMEM((nlev, cols, rows), f32),
            pltpu.VMEM((cols, rows), i32),
            pltpu.VMEM(weights.shape, bf16),
            pltpu.VMEM((ntr, 2, cols, rows), bf16),
            pltpu.VMEM((ntr, 2, cols, rows), bf16),
            pltpu.VMEM((ntr, 2, cols, rows), bf16),
            pltpu.VMEM((ntr, 2, cols, rows), bf16),
            pltpu.VMEM((cols, rows), f32),
            pltpu.VMEM((ntr, nlev, 8, rows), f32),
            pltpu.VMEM((ntr, nlev, 8, rows), f32),
            pltpu.VMEM((nlev, 8, rows), f32),
            pltpu.VMEM((8, rows), i32),
            pltpu.VMEM((8, rows), i32),
            pltpu.VMEM((cols, 128), f32),
            pltpu.VMEM((cols, 128), f32),
            pltpu.VMEM((cols, 128), f32),
            pltpu.VMEM((16, 8, 128), i32),
            pltpu.VMEM((16, 8, 128), i32),
            pltpu.VMEM((32, 128), i32),
            pltpu.SMEM((32, 128), i32),
            pltpu.VMEM(tracers.shape, f32),
            pltpu.VMEM((2, BLOCKS * SB // 128 * GROUP, 128), f32),
            pltpu.VMEM((2, BLOCKS, GROUP, SB), bf16),
            pltpu.VMEM((2, 2, 4, BLOCKS, GROUP, SB), bf16),
            pltpu.VMEM((PATTERNS * BLOCKS, GROUP, DB), bf16),
            pltpu.VMEM((16, 32 * GROUP, DB), bf16),
            pltpu.VMEM((2, 8, 8, 2 * GROUP, DB), bf16),
            pltpu.VMEM((16, height, 32 * GROUP), bf16),
            pltpu.VMEM((2, RING, height, DB), f32),
            pltpu.VMEM((2, 2, 4, height, DB), bf16),
            pltpu.VMEM((2, 2, 4, height, DB), bf16),
            dma((7,)),
            dma((messages,)),
            dma((messages,)),
            dma((2, 2, 14)),
            dma((2, 2, 14)),
            dma((2, 8)),
            dma((2, 8)),
            dma((2, 2, 4 * PARTS)),
            dma((2, 2, 4 * PARTS)),
        ],
        compiler_params=pltpu.CompilerParams(
            collective_id=1, has_side_effects=True, vmem_limit_bytes=54 * 1024 * 1024
        ),
        cost_estimate=pl.CostEstimate(flops=14_000_000_000, bytes_accessed=6_000_000, transcendentals=0),
    )(
        tracers, u_courant, v_courant, w_courant, land_mask, weights,
        *(a.reshape(1, -1) for a in (src_block, dst_tile, dst_block, pattern)),
    )
    results = (new_tracers, fields, fluxes)
    return tuple(pl.pallas_call(
        deliver,
        out_shape=[jax.ShapeDtypeStruct(a.shape, a.dtype) for a in results],
        in_specs=[vmem] * 3,
        out_specs=[anywhere] * 3,
        scratch_shapes=[dma((3,))],
    )(*results))


def solution(mesh):
    in_specs = (
        P(None, "lev", "tile", None),
        P("lev", "tile", None),
        P("lev", "tile", None),
        P("lev", "tile", None),
        P("tile", None),
        P(),
        P("tile"),
        P("tile", None),
        P("tile"),
        P("tile"),
    )
    out_specs = (P(None, "lev", "tile", None), P(None, "lev", "tile"), P(None, "lev", "tile"))
    return jax.shard_map(shards, mesh=mesh, in_specs=in_specs, out_specs=out_specs, check_vma=False)
```

time: 541 us -> 82 us (0.15)
  the two profiles are of different devices: /device:TPU:107 before, /device:TPU:1 now
where the time goes in v3:
time: 82 us; the launch traced here: 81.8 us
  Pallas kernels  81 us (99%)
    pallas_call x1, Pallas kernels, shards(): pl.pallas_call(kernel, out_shape=[jax.ShapeDtypeStruct(tracers.shape, f32...  78.7 us
    pallas_call x1, Pallas kernels, shards(): pl.pallas_call(deliver, out_shape=[jax.ShapeDtypeStruct(a.shape, a.dtype)...  2.34 us

profile of v3, /device:TPU:1, one launch (start us, length us, event | category | flops | bytes accessed | tf_op | source)
XLA Modules:
  0.0 81.8 jit_solution(7413950201890236462)
XLA Ops:
  0.6 78.7 %shard_map.121 = (f32[4,4,32,384]{3,2,1,0:T(8,128)}, f32[4,4,4096]{2,1,0:T(4,128)}, f32[4,4,4096]{2,1,0:T(4,128)}) custom-call(f32[4,4,32,384]{3,2,1,0:T(8,128)} %tr_hbm.1, f32[4,32,384]{2,1,0:T(8,128)} %u_hbm.1, f32[4,32,384]{2,1,0:T(8,128)} %v_hbm.1, f32[4,32,384]{2,1,0:T(8,128)} %w_hbm.1, s32[32,384]{1,0:T(8,128)} %land_hbm.1, ...), custom_call_target="tpu_custom_call" | custom-call | flops 14000000000 | bytes 6000000 | tf_op jit(solution)/shard_map/pallas_call | solution.py:454
  79.3 2.3 %shard_map.122 = (f32[4,4,32,384]{3,2,1,0:T(8,128)}, f32[4,4,4096]{2,1,0:T(4,128)}, f32[4,4,4096]{2,1,0:T(4,128)}) custom-call(f32[4,4,32,384]{3,2,1,0:T(8,128)} %get-tuple-element.6.new_in, f32[4,4,4096]{2,1,0:T(4,128)} %get-tuple-element.7.fields_in, f32[4,4,4096]{2,1,0:T(4,128)} %get-tuple-element.8.fluxes_in), custom_call_target="tpu_custom_call" | custom-call | tf_op jit(solution)/shard_map/pallas_call | solution.py:517

commit v4 on v3

--- a/solution.py
+++ b/solution.py
@@ -14,6 +14,7 @@
 DB = 256
 PATTERNS = 8
 SLOTS = 32
+QUARTERS = (1, 2, 0, 3)
 PARTS = 4
 HALVES = (range(0, PARTS // 2), range(PARTS // 2, PARTS))
 
@@ -61,10 +62,10 @@
 
 def kernel(
     tr_hbm, u_hbm, v_hbm, w_hbm, land_hbm, weights_hbm, src_ref, tile_ref, block_ref, pattern_ref,
-    new_ref, out0, out1,
+    new_hbm, out0, out1,
     tr, u_ref, v_ref, w_ref, land_ref, weights,
-    up_out, down_out, up_in, down_in, w_in, west_tr, east_tr, west_u, west_land, east_land,
-    fold_out, fold_in, mirrored, tab_src, tab_in, tab, tab_s, div, staged,
+    up_out, down_out, up_in, down_in, w_in, east_out, west_out, west_in, east_in,
+    fold_out, fold_in, mirrored, tab_src, tab_in, tab, tab_s, div, staged, new_ref,
     x_ref, ag, prod, terms, terms_out, masks, acc, rs_out, rs_in,
     load, send, recv, ag_send, ag_recv, sib_send, sib_recv, rs_send, rs_recv,
 ):
@@ -103,10 +104,7 @@
     for copy in loads[:5]:
         copy.start()
     slot_tables(tab_src, y, z, c, src_ref, tile_ref, block_ref, pattern_ref)
-    loads[0].wait()
-    down_out[...] = tr[:, 0:2].astype(jnp.bfloat16)
-    up_out[...] = tr[:, nlev - 2 : nlev].astype(jnp.bfloat16)
-    for n in range(1, 5):
+    for n in range(5):
         loads[n].wait()
     lane = lax.broadcasted_iota(jnp.int32, (cols, 128), 1)
     top = rows - 128
@@ -121,6 +119,21 @@
     ocean = land_ref[...].astype(jnp.float32)
     packed = jnp.where(lane == first + nlev, pltpu.roll(ocean[:, top:], first + nlev + 1, 1), packed)
     fold_out[...] = packed
+    last = cols - 8
+    east_out[first : first + 8, :] = jnp.zeros((8, rows), jnp.float32)
+    west_out[first : first + 8, :] = jnp.zeros((8, rows), jnp.float32)
+    for q in range(ntr * nlev):
+        east_out[2 * q : 2 * q + 2, :] = tr[q // nlev, q % nlev, cols - 2 : cols, :]
+        west_out[2 * q : 2 * q + 2, :] = tr[q // nlev, q % nlev, 0:2, :]
+    for k in range(nlev):
+        east_out[first + k : first + k + 1, :] = u_ref[k, cols - 1 : cols, :]
+    east_out[first + nlev : first + nlev + 1, :] = ocean[cols - 1 : cols]
+    west_out[first + nlev : first + nlev + 1, :] = ocean[0:1]
+    for n in QUARTERS:
+        for t in range(ntr):
+            for out, k in ((down_out, 0), (up_out, nlev - 2)):
+                two = [tr[t, k + m, n * 8 : n * 8 + 8, :] for m in range(2)]
+                out[n, t * 16 : t * 16 + 16, :] = jnp.concatenate(two, 0).astype(jnp.bfloat16)
     pl.semaphore_wait(barrier, len(partners))
 
     copies = []
@@ -138,22 +151,20 @@
         start(copies[-1])
         return copies[-1]
 
-    last, middle = cols - 8, cols // 2
     sent_fold = [send_to(fold_out, fold_in, fold)]
-    sent_side = [
-        send_to(tr.at[:, :, pl.ds(last, 8)], west_tr, east),
-        send_to(tr.at[:, :, pl.ds(0, 8)], east_tr, west),
-        send_to(u_ref.at[:, pl.ds(last, 8)], west_u, east),
-        send_to(land_ref.at[pl.ds(last, 8)], west_land, east),
-        send_to(land_ref.at[pl.ds(0, 8)], east_land, west),
-    ]
-    sent_lev = []
-    for at in (pl.ds(0, middle), pl.ds(middle, middle)):
-        sent_lev.append([
-            send_to(up_out.at[:, :, at], up_in.at[:, :, at], below),
-            send_to(down_out.at[:, :, at], down_in.at[:, :, at], above),
+
+    def send_levels(n):
+        at = pl.ds(n * 8, 8)
+        return [
+            send_to(up_out.at[n], up_in.at[n], below),
+            send_to(down_out.at[n], down_in.at[n], above),
             send_to(w_ref.at[nlev - 1, at], w_in.at[at], below),
-        ])
+        ]
+
+    sent_lev = {QUARTERS[0]: send_levels(QUARTERS[0])}
+    sent_side = [send_to(east_out, west_in, east), send_to(west_out, east_in, west)]
+    for n in QUARTERS[1:]:
+        sent_lev[n] = send_levels(n)
     sent_table = [
         send_to(tab_src.at[h * 8 + row], tab_in.at[h * 8 + NEAR[o]], other) for o, h, row, other in table_to
     ]
@@ -166,30 +177,41 @@
     def behind(a, axis):
         return pltpu.roll(a, 1, axis)
 
-    for copy in sent_side:
-        copy.wait_recv()
-    ocean_tall = jnp.concatenate(
-        [west_land[...].astype(jnp.float32), ocean, east_land[...].astype(jnp.float32)], 0
-    )
-    open_east = ocean_tall * ahead(ocean_tall, 0)
-    for k in range(nlev):
-        courant = jnp.concatenate([west_u[k], u_ref[k], jnp.zeros((8, rows), jnp.float32)], 0)
-        coefs = coefficients(courant, open_east)
-        for t in range(ntr):
-            x = jnp.concatenate([west_tr[t, k], tr[t, k], east_tr[t, k]], 0)
-            beyond = ahead(x, 0)
-            step = beyond - x
-            slope = minmod(behind(step, 0), step)
-            out = flux(coefs, x, slope, beyond, ahead(slope, 0))
-            div[t, k] = (out - behind(out, 0))[8 : 8 + cols]
-
-    for copy in sent_table:
-        copy.wait_recv()
-    for h, row in ((0, z), (1, y)):
-        tab[h * 8 : h * 8 + 1, :] = tab_src[h * 8 + row, 0:1, :]
-        for j in range(1, 8):
-            tab[h * 8 + j : h * 8 + j + 1, :] = tab_in[h * 8 + j, 0:1, :]
-    sent_tables = send_to(tab.at[pl.ds(0, 16)], tab.at[pl.ds(16, 16)], sibling)
+    def east_part(cells, courants, mask, columns, at):
+        opening = mask * ahead(mask, 0)
+        for k in range(nlev):
+            coefs = coefficients(courants(k), opening)
+            for t in range(ntr):
+                x = cells(t, k)
+                beyond = ahead(x, 0)
+                step = beyond - x
+                slope = minmod(behind(step, 0), step)
+                out = flux(coefs, x, slope, beyond, ahead(slope, 0))
+                div[t, k, columns, :] = (out - behind(out, 0))[at]
+
+    inner = slice(8, cols - 8)
+    east_part(lambda t, k: tr[t, k], lambda k: u_ref[k], ocean, inner, inner)
+
+    def unpacked(packed_ref, row, at):
+        tile = packed_ref[row // 8 * 8 : row // 8 * 8 + 8, :]
+        turn = (at - row) % 8
+        return pltpu.roll(tile, turn, 0) if turn else tile
+
+    def east_ends(n):
+        if n == 0:
+            mask = jnp.concatenate([unpacked(west_in, first + nlev, 7), ocean[:16]], 0)
+            east_part(
+                lambda t, k: jnp.concatenate([unpacked(west_in, 2 * (t * nlev + k), 6), tr[t, k, :16, :]], 0),
+                lambda k: jnp.concatenate([unpacked(west_in, first + k, 7), u_ref[k, :16, :]], 0),
+                mask, slice(0, 8), slice(8, 16),
+            )
+        else:
+            mask = jnp.concatenate([ocean[cols - 16 :], unpacked(east_in, first + nlev, 0)], 0)
+            east_part(
+                lambda t, k: jnp.concatenate([tr[t, k, cols - 16 :, :], unpacked(east_in, 2 * (t * nlev + k), 0)], 0),
+                lambda k: jnp.concatenate([u_ref[k, cols - 16 :, :], jnp.zeros((8, rows), jnp.float32)], 0),
+                mask, slice(last, cols), slice(8, 16),
+            )
 
     for copy in sent_fold:
         copy.wait_recv()
@@ -222,9 +244,9 @@
     quarter = BLOCKS // 4
 
     def gather_copy(h, d, n):
-        k, sub = (n // 4 + 1, n % 4) if n < 12 else (4, 2 * d + n - 12)
-        blocks = pl.ds(quarter * sub, quarter)
-        src = x_ref.at[h, blocks] if k == 1 else ag.at[h, d, k - 2, blocks]
+        k, at = (n // 4 + 1, n % 4) if n < 12 else (4, 2 * (n - 12) + d)
+        blocks = pl.ds(quarter * at, quarter)
+        src = x_ref.at[h, pl.ds(quarter * QUARTERS[at], quarter)] if k == 1 else ag.at[h, d, k - 2, blocks]
         dst = ag.at[h, 0 if k == 4 else d, k - 1, blocks]
         return pltpu.make_async_remote_copy(
             src_ref=src, dst_ref=dst, send_sem=ag_send.at[h, d, n], recv_sem=ag_recv.at[h, d, n],
@@ -234,20 +256,26 @@
     not_first = jnp.where(lev > 0, 1.0, 0.0).astype(jnp.float32)
     not_last = jnp.where(lev < levs - 1, 1.0, 0.0).astype(jnp.float32)
     across = rows // 128
-    for i0 in range(0, cols, 8):
+    for turn, quarter_at in enumerate(QUARTERS):
+        i0 = quarter_at * 8
         part = slice(i0, i0 + 8)
+        if turn == 2:
+            for copy in sent_side:
+                copy.wait_recv()
+        if turn >= 2:
+            east_ends(quarter_at)
         north_part(part)
-        if i0 % middle == 0:
-            for copy in sent_lev[i0 // middle]:
-                copy.wait_recv()
+        for copy in sent_lev[quarter_at]:
+            copy.wait_recv()
         open_part = land_ref[part, :].astype(jnp.float32)
         coefs = [coefficients(w_in[part, :], open_part * not_first)]
         for k in range(nlev):
             coefs.append(coefficients(w_ref[k, part, :], open_part * not_last if k == nlev - 1 else open_part))
         for t in range(ntr):
-            cells = [up_in[t, m, part, :].astype(jnp.float32) * not_first for m in range(2)]
+            beneath, over = (a[quarter_at, t * 16 : t * 16 + 16, :].astype(jnp.float32) for a in (down_in, up_in))
+            cells = [over[:8] * not_first, over[8:] * not_first]
             cells += [tr[t, k, part, :] for k in range(nlev)]
-            cells += [down_in[t, m, part, :].astype(jnp.float32) * not_last for m in range(2)]
+            cells += [beneath[:8] * not_last, beneath[8:] * not_last]
             steps = [b - a for a, b in zip(cells[:-1], cells[1:])]
             slopes = [minmod(a, b) for a, b in zip(steps[:-1], steps[1:])]
             faces = [
@@ -268,12 +296,10 @@
                     at = (b * (SB // 128) + m) * GROUP
                     x_ref[kind, b, :, m * 128 : m * 128 + 128] = staged[kind, at : at + GROUP, :].astype(jnp.bfloat16)
         for h, d in streams:
-            start(gather_copy(h, d, i0 // 8))
-
-    sent_tables.wait_recv()
-    to_scalars = pltpu.make_async_copy(tab, tab_s, load.at[6])
-    to_scalars.start()
-    to_scalars.wait()
+            start(gather_copy(h, d, turn))
+    new_copy = pltpu.make_async_copy(new_ref, new_hbm, load.at[7])
+    new_copy.start()
+
     lanes = 2 * 8 * 2 * GROUP
     sub_i = lax.broadcasted_iota(jnp.int32, (NBD * GROUP, lanes), 0)
     lane_i = lax.broadcasted_iota(jnp.int32, (NBD * GROUP, lanes), 1)
@@ -291,8 +317,6 @@
         masks[i] = jnp.where(blocks == wanted, 1.0, 0.0).astype(jnp.bfloat16)
         return carry
 
-    lax.fori_loop(0, 16, one_mask, 0)
-    loads[5].wait()
 
     def sibling_copy(h, j):
         at = pl.ds((8 + j) * 2 * GROUP, 2 * GROUP)
@@ -301,20 +325,23 @@
             send_sem=sib_send.at[h, j], recv_sem=sib_recv.at[h, j], device_id=sibling, device_id_type=MESH,
         )
 
-    def multiply(view, b0, count):
-        x = view[b0 : b0 + count].reshape(count * GROUP, SB)
+    def multiply(at, view, first_quarter, places):
+        count = quarter * len(places)
+        x = view[quarter * first_quarter : quarter * first_quarter + count].reshape(count * GROUP, SB)
 
         def one_pattern(p, carry):
             r = jnp.dot(x, weights[p], preferred_element_type=jnp.float32)
-            prod[pl.ds(p * BLOCKS + b0, count)] = r.astype(jnp.bfloat16).reshape(count, GROUP, DB)
+            r = r.astype(jnp.bfloat16).reshape(count, GROUP, DB)
+            for i, place in enumerate(places):
+                prod[at, pl.ds(p * BLOCKS + quarter * place, quarter)] = r[i * quarter : (i + 1) * quarter]
             return carry
 
         lax.fori_loop(0, PATTERNS, one_pattern, 0, unroll=PATTERNS)
 
-    def pick(h, j):
+    def pick(h, j, at):
         def product(slot):
             src, pat = tab_s[h * 8 + j, slot], tab_s[h * 8 + j, SLOTS + slot]
-            return prod[jnp.clip(pat * BLOCKS + src, 0, PATTERNS * BLOCKS - 1)]
+            return prod[at, jnp.clip(pat * BLOCKS + src, 0, PATTERNS * BLOCKS - 1)]
 
         def one_target(q, carry):
             for r in range(2):
@@ -327,32 +354,59 @@
         lax.fori_loop(0, 8, one_target, 0, unroll=4)
         start(sibling_copy(h, j))
 
-    def arrived(h, j):
-        k, d = (j + 1) // 2, (j + 1) % 2
-        multiply(x_ref.at[h] if j == 0 else ag.at[h, d, k - 1], 0, BLOCKS)
-        pick(h, j)
-
-    waiting = [(0, 0), (1, 0)]
+    def own(h):
+        multiply(h * 2, x_ref.at[h], 0, range(4))
+        pick(h, 0, h * 2)
+
+    def whole(k, h, d):
+        multiply(h * 2 + d, ag.at[h, d, k - 1], 0, QUARTERS)
+        pick(h, 2 * k - 1 + d, h * 2 + d)
+
+    def early(k, h, d):
+        multiply(h * 2 + d, ag.at[h, d, k - 1], 0, QUARTERS[:2])
+
+    def late(k, h, d):
+        multiply(h * 2 + d, ag.at[h, d, k - 1], 2, QUARTERS[2:])
+        pick(h, 2 * k - 1 + d, h * 2 + d)
+
+    waiting = [(own, 0), (own, 1)]
+    todo = {3: (whole, 1), 5: (early, 2), 7: (late, 2), 9: (early, 3), 11: (late, 3)}
     for n in range(12):
         for h, d in streams:
             gather_copy(h, d, n).wait_recv()
             if n < 8:
                 start(gather_copy(h, d, n + 4))
-            elif (n - 8) // 2 == d:
-                start(gather_copy(h, d, 12 + (n - 8) % 2))
-        if waiting:
-            arrived(*waiting.pop(0))
-        if n % 4 == 3:
-            k = n // 4 + 1
-            waiting += [(0, 2 * k - 1), (0, 2 * k), (1, 2 * k - 1), (1, 2 * k)]
-    while waiting:
-        arrived(*waiting.pop(0))
-    for h in range(2):
-        for n in (12, 13):
+            elif n % 2 == d:
+                start(gather_copy(h, d, 12 + (n - 8) // 2))
+        if n == 0:
+            for copy in sent_table:
+                copy.wait_recv()
+            for h, row in ((0, z), (1, y)):
+                tab[h * 8 : h * 8 + 1, :] = tab_src[h * 8 + row, 0:1, :]
+                for j in range(1, 8):
+                    tab[h * 8 + j : h * 8 + j + 1, :] = tab_in[h * 8 + j, 0:1, :]
+            sent_tables = send_to(tab.at[pl.ds(0, 16)], tab.at[pl.ds(16, 16)], sibling)
+
+        elif n == 1:
+            sent_tables.wait_recv()
+            to_scalars = pltpu.make_async_copy(tab, tab_s, load.at[6])
+            to_scalars.start()
+            to_scalars.wait()
+            lax.fori_loop(0, 16, one_mask, 0)
+            loads[5].wait()
+        for _ in range(2 if n > 1 else 0):
+            if waiting:
+                work, *of = waiting.pop(0)
+                work(*of)
+        if n in todo:
+            waiting += [(*todo[n], h, d) for h, d in streams]
+    for work, *of in waiting:
+        work(*of)
+    for n, work in ((12, early), (13, late)):
+        for h in range(2):
             for d in range(2):
                 gather_copy(h, d, n).wait_recv()
-        multiply(ag.at[h, 0, 3], 0, BLOCKS)
-        pick(h, 7)
+            work(4, h, 0)
 
     size = NBD * GROUP // PARTS
 
@@ -419,16 +473,22 @@
                 for t in range(ntr):
                     at_row = i * GROUP + t * nlev
                     out[t, :, b * DB : (b + 1) * DB] = total[at_row : at_row + nlev]
+    new_copy.wait()
     for copy in started:
         copy.wait_send()
 
 
-def deliver(new_in, fields_in, fluxes_in, new_out, fields_out, fluxes_out, done):
-    pairs = ((new_in, new_out), (fields_in, fields_out), (fluxes_in, fluxes_out))
-    copies = [pltpu.make_async_copy(src, dst, done.at[n]) for n, (src, dst) in enumerate(pairs)]
-    for copy in copies:
+def deliver(new_in, fields_in, fluxes_in, new_out, fields_out, fluxes_out, new, fields, fluxes, load, store):
+    pieces = [(fields_in, fields, fields_out), (fluxes_in, fluxes, fluxes_out)]
+    pieces += [(new_in.at[t], new.at[t], new_out.at[t]) for t in range(new.shape[0])]
+    loads = [pltpu.make_async_copy(src, held, load.at[n]) for n, (src, held, _) in enumerate(pieces)]
+    stores = [pltpu.make_async_copy(held, dst, store.at[n]) for n, (_, held, dst) in enumerate(pieces)]
+    for copy in loads:
         copy.start()
-    for copy in copies:
+    for arriving, leaving in zip(loads, stores):
+        arriving.wait()
+        leaving.start()
+    for copy in stores:
         copy.wait()
 
 
@@ -450,7 +510,7 @@
     ntr, nlev, cols, rows = tracers.shape
     height = NBD * GROUP
     dma = pltpu.SemaphoreType.DMA
-    messages = 1 + 5 + 6 + 14 + 1
+    messages = 1 + 2 + 12 + 14 + 1
     new_tracers, fields, fluxes = pl.pallas_call(
         kernel,
         out_shape=[
@@ -459,7 +519,7 @@
             jax.ShapeDtypeStruct((ntr, nlev, NBD * DB), f32),
         ],
         in_specs=[anywhere] * 6 + [vmem] * 4,
-        out_specs=[vmem] * 3,
+        out_specs=[anywhere, vmem, vmem],
         scratch_shapes=[
             pltpu.VMEM(tracers.shape, f32),
             pltpu.VMEM((nlev, cols, rows), f32),
@@ -467,16 +527,15 @@
             pltpu.VMEM((nlev, cols, rows), f32),
             pltpu.VMEM((cols, rows), i32),
             pltpu.VMEM(weights.shape, bf16),
-            pltpu.VMEM((ntr, 2, cols, rows), bf16),
-            pltpu.VMEM((ntr, 2, cols, rows), bf16),
-            pltpu.VMEM((ntr, 2, cols, rows), bf16),
-            pltpu.VMEM((ntr, 2, cols, rows), bf16),
+            pltpu.VMEM((4, ntr * 16, rows), bf16),
+            pltpu.VMEM((4, ntr * 16, rows), bf16),
+            pltpu.VMEM((4, ntr * 16, rows), bf16),
+            pltpu.VMEM((4, ntr * 16, rows), bf16),
             pltpu.VMEM((cols, rows), f32),
-            pltpu.VMEM((ntr, nlev, 8, rows), f32),
-            pltpu.VMEM((ntr, nlev, 8, rows), f32),
-            pltpu.VMEM((nlev, 8, rows), f32),
-            pltpu.VMEM((8, rows), i32),
-            pltpu.VMEM((8, rows), i32),
+            pltpu.VMEM((2 * ntr * nlev + 8, rows), f32),
+            pltpu.VMEM((2 * ntr * nlev + 8, rows), f32),
+            pltpu.VMEM((2 * ntr * nlev + 8, rows), f32),
+            pltpu.VMEM((2 * ntr * nlev + 8, rows), f32),
             pltpu.VMEM((cols, 128), f32),
             pltpu.VMEM((cols, 128), f32),
             pltpu.VMEM((cols, 128), f32),
@@ -486,16 +545,17 @@
             pltpu.SMEM((32, 128), i32),
             pltpu.VMEM(tracers.shape, f32),
             pltpu.VMEM((2, BLOCKS * SB // 128 * GROUP, 128), f32),
+            pltpu.VMEM(tracers.shape, f32),
             pltpu.VMEM((2, BLOCKS, GROUP, SB), bf16),
             pltpu.VMEM((2, 2, 4, BLOCKS, GROUP, SB), bf16),
-            pltpu.VMEM((PATTERNS * BLOCKS, GROUP, DB), bf16),
+            pltpu.VMEM((4, PATTERNS * BLOCKS, GROUP, DB), bf16),
             pltpu.VMEM((16, 32 * GROUP, DB), bf16),
             pltpu.VMEM((2, 8, 8, 2 * GROUP, DB), bf16),
             pltpu.VMEM((16, height, 32 * GROUP), bf16),
             pltpu.VMEM((2, RING, height, DB), f32),
             pltpu.VMEM((2, 2, 4, height, DB), bf16),
             pltpu.VMEM((2, 2, 4, height, DB), bf16),
-            dma((7,)),
+            dma((8,)),
             dma((messages,)),
             dma((messages,)),
             dma((2, 2, 14)),
@@ -517,9 +577,10 @@
     return tuple(pl.pallas_call(
         deliver,
         out_shape=[jax.ShapeDtypeStruct(a.shape, a.dtype) for a in results],
-        in_specs=[vmem] * 3,
+        in_specs=[anywhere] * 3,
         out_specs=[anywhere] * 3,
-        scratch_shapes=[dma((3,))],
+        scratch_shapes=[pltpu.VMEM(a.shape, a.dtype) for a in results] + [dma((2 + ntr,)), dma((2 + ntr,))],
+        compiler_params=pltpu.CompilerParams(vmem_limit_bytes=54 * 1024 * 1024),
     )(*results))
 
 

time: 82 us -> 78.7 us (0.960)
  Pallas kernels: 81 us -> 77.5 us
    pallas_call x1, Pallas kernels: 78.7 us -> 75.4 us  [shards(): pl.pallas_call(kernel, out_shape=[jax.ShapeDtypeStruct(tracers.shape, f32...]
where the time goes in v4:
time: 78.7 us; the launch traced here: 78.4 us
  Pallas kernels  77.5 us (98%)
  between operations  0.82 us (1%)
    pallas_call x1, Pallas kernels, shards(): pl.pallas_call(kernel, out_shape=[jax.ShapeDtypeStruct(tracers.shape, f32...  75.4 us
    pallas_call x1, Pallas kernels, shards(): pl.pallas_call(deliver, out_shape=[jax.ShapeDtypeStruct(a.shape, a.dtype)...  2.1 us

profile of v4, /device:TPU:1, one launch (start us, length us, event | category | flops | bytes accessed | tf_op | source)
XLA Modules:
  0.0 78.4 jit_solution(9054290189649634986)
XLA Ops:
  0.6 75.4 %shard_map.121 = (f32[4,4,32,384]{3,2,1,0:T(8,128)}, f32[4,4,4096]{2,1,0:T(4,128)}, f32[4,4,4096]{2,1,0:T(4,128)}) custom-call(f32[4,4,32,384]{3,2,1,0:T(8,128)} %tr_hbm.1, f32[4,32,384]{2,1,0:T(8,128)} %u_hbm.1, f32[4,32,384]{2,1,0:T(8,128)} %v_hbm.1, f32[4,32,384]{2,1,0:T(8,128)} %w_hbm.1, s32[32,384]{1,0:T(8,128)} %land_hbm.1, ...), custom_call_target="tpu_custom_call" | custom-call | flops 14000000000 | bytes 6000000 | tf_op jit(solution)/shard_map/pallas_call | solution.py:514
  76.1 2.1 %shard_map.122 = (f32[4,4,32,384]{3,2,1,0:T(8,128)}, f32[4,4,4096]{2,1,0:T(4,128)}, f32[4,4,4096]{2,1,0:T(4,128)}) custom-call(f32[4,4,32,384]{3,2,1,0:T(8,128)} %get-tuple-element.6.new_in, f32[4,4,4096]{2,1,0:T(4,128)} %get-tuple-element.7.fields_in, f32[4,4,4096]{2,1,0:T(4,128)} %get-tuple-element.8.fluxes_in), custom_call_target="tpu_custom_call" | custom-call | tf_op jit(solution)/shard_map/pallas_call | solution.py:577

commit v5 on v4

--- a/solution.py
+++ b/solution.py
@@ -104,7 +104,42 @@
     for copy in loads[:5]:
         copy.start()
     slot_tables(tab_src, y, z, c, src_ref, tile_ref, block_ref, pattern_ref)
-    for n in range(5):
+    loads[0].wait()
+    def cast(n):
+        for t in range(ntr):
+            for out, k in ((down_out, 0), (up_out, nlev - 2)):
+                two = [tr[t, k + m, n * 8 : n * 8 + 8, :] for m in range(2)]
+                out[n, t * 16 : t * 16 + 16, :] = jnp.concatenate(two, 0).astype(jnp.bfloat16)
+
+    cast(QUARTERS[0])
+    loads[4].wait()
+    pl.semaphore_wait(barrier, len(partners))
+
+    copies = []
+    started = []
+
+    def start(copy):
+        copy.start()
+        started.append(copy)
+
+    def send_to(src, dst, other):
+        n = len(copies)
+        copies.append(pltpu.make_async_remote_copy(
+            src_ref=src, dst_ref=dst, send_sem=send.at[n], recv_sem=recv.at[n], device_id=other, device_id_type=MESH,
+        ))
+        start(copies[-1])
+        return copies[-1]
+
+    def send_levels(n):
+        at = pl.ds(n * 8, 8)
+        return [
+            send_to(up_out.at[n], up_in.at[n], below),
+            send_to(down_out.at[n], down_in.at[n], above),
+            send_to(w_ref.at[nlev - 1, at], w_in.at[at], below),
+        ]
+
+    sent_lev = {QUARTERS[0]: send_levels(QUARTERS[0])}
+    for n in range(1, 4):
         loads[n].wait()
     lane = lax.broadcasted_iota(jnp.int32, (cols, 128), 1)
     top = rows - 128
@@ -119,6 +154,10 @@
     ocean = land_ref[...].astype(jnp.float32)
     packed = jnp.where(lane == first + nlev, pltpu.roll(ocean[:, top:], first + nlev + 1, 1), packed)
     fold_out[...] = packed
+    sent_fold = [send_to(fold_out, fold_in, fold)]
+    for n in QUARTERS[1:]:
+        cast(n)
+        sent_lev[n] = send_levels(n)
     last = cols - 8
     east_out[first : first + 8, :] = jnp.zeros((8, rows), jnp.float32)
     west_out[first : first + 8, :] = jnp.zeros((8, rows), jnp.float32)
@@ -129,42 +168,7 @@
         east_out[first + k : first + k + 1, :] = u_ref[k, cols - 1 : cols, :]
     east_out[first + nlev : first + nlev + 1, :] = ocean[cols - 1 : cols]
     west_out[first + nlev : first + nlev + 1, :] = ocean[0:1]
-    for n in QUARTERS:
-        for t in range(ntr):
-            for out, k in ((down_out, 0), (up_out, nlev - 2)):
-                two = [tr[t, k + m, n * 8 : n * 8 + 8, :] for m in range(2)]
-                out[n, t * 16 : t * 16 + 16, :] = jnp.concatenate(two, 0).astype(jnp.bfloat16)
-    pl.semaphore_wait(barrier, len(partners))
-
-    copies = []
-    started = []
-
-    def start(copy):
-        copy.start()
-        started.append(copy)
-
-    def send_to(src, dst, other):
-        n = len(copies)
-        copies.append(pltpu.make_async_remote_copy(
-            src_ref=src, dst_ref=dst, send_sem=send.at[n], recv_sem=recv.at[n], device_id=other, device_id_type=MESH,
-        ))
-        start(copies[-1])
-        return copies[-1]
-
-    sent_fold = [send_to(fold_out, fold_in, fold)]
-
-    def send_levels(n):
-        at = pl.ds(n * 8, 8)
-        return [
-            send_to(up_out.at[n], up_in.at[n], below),
-            send_to(down_out.at[n], down_in.at[n], above),
-            send_to(w_ref.at[nlev - 1, at], w_in.at[at], below),
-        ]
-
-    sent_lev = {QUARTERS[0]: send_levels(QUARTERS[0])}
     sent_side = [send_to(east_out, west_in, east), send_to(west_out, east_in, west)]
-    for n in QUARTERS[1:]:
-        sent_lev[n] = send_levels(n)
     sent_table = [
         send_to(tab_src.at[h * 8 + row], tab_in.at[h * 8 + NEAR[o]], other) for o, h, row, other in table_to
     ]

time: 78.7 us -> 78.9 us (level)
  no operation moved by 1% of the time
where the time goes in v5:
time: 78.9 us; the launch traced here: 78.6 us
  Pallas kernels  77.8 us (99%)
  between operations  0.82 us (1%)
    pallas_call x1, Pallas kernels, shards(): pl.pallas_call(kernel, out_shape=[jax.ShapeDtypeStruct(tracers.shape, f32...  75.7 us
    pallas_call x1, Pallas kernels, shards(): pl.pallas_call(deliver, out_shape=[jax.ShapeDtypeStruct(a.shape, a.dtype)...  2.1 us

profile of v5, /device:TPU:1, one launch (start us, length us, event | category | flops | bytes accessed | tf_op | source)
XLA Modules:
  0.0 78.6 jit_solution(11943644973381145837)
XLA Ops:
  0.6 75.7 %shard_map.121 = (f32[4,4,32,384]{3,2,1,0:T(8,128)}, f32[4,4,4096]{2,1,0:T(4,128)}, f32[4,4,4096]{2,1,0:T(4,128)}) custom-call(f32[4,4,32,384]{3,2,1,0:T(8,128)} %tr_hbm.1, f32[4,32,384]{2,1,0:T(8,128)} %u_hbm.1, f32[4,32,384]{2,1,0:T(8,128)} %v_hbm.1, f32[4,32,384]{2,1,0:T(8,128)} %w_hbm.1, s32[32,384]{1,0:T(8,128)} %land_hbm.1, ...), custom_call_target="tpu_custom_call" | custom-call | flops 14000000000 | bytes 6000000 | tf_op jit(solution)/shard_map/pallas_call | solution.py:518
  76.3 2.1 %shard_map.122 = (f32[4,4,32,384]{3,2,1,0:T(8,128)}, f32[4,4,4096]{2,1,0:T(4,128)}, f32[4,4,4096]{2,1,0:T(4,128)}) custom-call(f32[4,4,32,384]{3,2,1,0:T(8,128)} %get-tuple-element.6.new_in, f32[4,4,4096]{2,1,0:T(4,128)} %get-tuple-element.7.fields_in, f32[4,4,4096]{2,1,0:T(4,128)} %get-tuple-element.8.fluxes_in), custom_call_target="tpu_custom_call" | custom-call | tf_op jit(solution)/shard_map/pallas_call | solution.py:581
